TPU v7x, 512 devices: a whole 4x8x8 slice. The times are simulated.
512 devices in a mesh: seq: 64 (over z, y), ch: 8 (over x, core).
Axes of the slice: x: 4, y: 8, z: 8, core: 2. Of those that a mesh axis runs over, the one named last changes fastest.
Arguments:
- upstream_grad: bfloat16 [8192, 4096], P('seq', 'ch'), may hold values from -6 to 6
- gate_act: bfloat16 [8192, 4096], P('seq', 'ch'), may hold values from -6 to 6
- value_act: bfloat16 [8192, 4096], P('seq', 'ch'), may hold values from -0.5 to 0.5
- filter_taps: bfloat16 [4, 8192], P(None, 'seq'), may hold values from -6 to 6
- half_ids: int32 [128], replicated, may hold values from 0 to 127, as said below
Outputs:
- value_grad: bfloat16 [8192, 4096], P('seq', 'ch')
- filter_grad: float32 [4, 8192], P(None, 'seq')
Inputs may be any that keep to these rules, and one draw needn't show every extreme that they name: `half_ids`: each value appears once; entries 2p and 2p + 1 add up to 127.
All inputs are finite; a program needn't handle non-finite values.
Results may differ from a plain program's by a relative error of at most 0.0049.
Values may be sent and summed in bfloat16 or wider, within the bound.
A program may use at most 128 MiB of HBM per device.

v0:
```python
import math

import jax
import jax.numpy as jnp
from jax import lax
from jax.sharding import PartitionSpec as P


def toeplitz_panel(segment, row_count, col_count):
    seg_len = segment.shape[-1]
    leading = segment.shape[:-1]
    repeated = jnp.tile(segment, (1,) * len(leading) + (row_count + 1,))
    needed = row_count * (seg_len - 1)
    flat_part = lax.slice_in_dim(repeated, row_count - 1, row_count - 1 + needed, axis=len(leading))
    return flat_part.reshape(leading + (row_count, seg_len - 1))[..., :col_count]


def skewed_sums(matrix):
    row_count = matrix.shape[-2]
    col_count = matrix.shape[-1]
    leading = matrix.shape[:-2]
    widened = jnp.pad(matrix, [(0, 0)] * len(leading) + [(0, 0), (0, row_count)])
    flat_part = widened.reshape(leading + (row_count * (col_count + row_count),))
    skewed = flat_part[..., : row_count * (col_count + row_count - 1)].reshape(
        leading + (row_count, col_count + row_count - 1)
    )
    return skewed.sum(-2)


def local(upstream_grad, gate_act, value_act, filter_taps, half_ids):
    local_rows, channels = upstream_grad.shape
    seq_count = lax.axis_size("seq")
    per_device = channels // seq_count
    filters = filter_taps.shape[0]
    copies = per_device // filters
    halves = 2 * seq_count
    half_rows = local_rows // 2
    total_rows = local_rows * seq_count

    def to_columns(array):
        return jnp.transpose(array.reshape(local_rows, seq_count, per_device), (1, 2, 0))

    exchanged = (
        lax.all_to_all(to_columns(upstream_grad), "seq", split_axis=0, concat_axis=2, tiled=True),
        lax.all_to_all(to_columns(gate_act), "seq", split_axis=0, concat_axis=2, tiled=True),
        lax.all_to_all(to_columns(value_act), "seq", split_axis=0, concat_axis=2, tiled=True),
    )
    grad_cols = (exchanged[0].astype(jnp.float32) * exchanged[1].astype(jnp.float32)).astype(
        jnp.bfloat16
    )
    value_cols = exchanged[2]
    whole_taps = lax.all_gather(filter_taps, "seq", axis=1, tiled=True)
    inverse = jnp.zeros((halves,), jnp.int32).at[half_ids].set(jnp.arange(halves, dtype=jnp.int32))

    def to_blocks(columns):
        ordered = jnp.take(columns.reshape(per_device, halves, half_rows), inverse, axis=1)
        return jnp.transpose(ordered.reshape(copies, filters, total_rows), (1, 0, 2))

    grad_global = to_blocks(grad_cols)
    value_global = to_blocks(value_cols)
    block_rows = 128
    blocks = total_rows // block_rows
    groups = min(2, blocks)
    group_span = blocks // groups
    span_cols = group_span * block_rows
    grad_blocks = grad_global.reshape(filters, copies, blocks, block_rows)
    value_reversed = jnp.flip(value_global.reshape(filters, copies, blocks, block_rows), 3)
    grad_padded = jnp.concatenate(
        [grad_blocks, jnp.zeros((filters, copies, group_span, block_rows), jnp.bfloat16)], 2
    )
    taps_padded = jnp.concatenate([jnp.zeros((filters, block_rows), jnp.bfloat16), whole_taps], 1)
    input_acc = jnp.zeros((filters, copies, blocks, block_rows), jnp.float32)
    lag_acc = jnp.zeros((filters, total_rows + block_rows - 1), jnp.float32)
    for group_index in range(groups):
        first_block = group_index * group_span
        live_rows = blocks - first_block
        hankel = jnp.concatenate(
            [
                grad_padded[:, :, first_block + offset : first_block + offset + live_rows, :]
                for offset in range(group_span)
            ],
            3,
        )
        start_lag = first_block * block_rows
        segment = taps_padded[:, start_lag + 1 : start_lag + span_cols + block_rows]
        toeplitz = toeplitz_panel(segment, block_rows, span_cols)
        product_part = jnp.einsum(
            "faiu,fru->fair", hankel, toeplitz, preferred_element_type=jnp.float32
        )
        input_acc = input_acc + jnp.pad(
            product_part, ((0, 0), (0, 0), (0, blocks - live_rows), (0, 0))
        )
        lag_matrix = jnp.einsum(
            "fair,faiu->fru",
            value_reversed[:, :, :live_rows],
            hankel,
            preferred_element_type=jnp.float32,
        )
        lag_acc = lag_acc.at[:, start_lag : start_lag + span_cols + block_rows - 1].add(
            skewed_sums(lag_matrix)
        )
    norm_scale = 1.0 / math.sqrt(total_rows)
    input_cols = (
        jnp.transpose(input_acc * norm_scale, (1, 0, 2, 3))
        .reshape(per_device, halves, half_rows)
        .astype(jnp.bfloat16)
    )
    slot_cols = jnp.take(input_cols, half_ids, axis=1).reshape(per_device, seq_count, local_rows)
    returned = lax.all_to_all(slot_cols, "seq", split_axis=1, concat_axis=0, tiled=True)
    value_grad = jnp.transpose(returned.reshape(channels, local_rows), (1, 0))
    lag_part = lag_acc[:, block_rows - 1 : block_rows - 1 + total_rows] * norm_scale
    reduced = lax.psum_scatter(lag_part, "seq", scatter_dimension=1, tiled=True)
    filter_grad = lax.psum(reduced, "ch")
    return (value_grad, filter_grad)


def solution(mesh):
    placed = (P("seq", "ch"), P("seq", "ch"), P("seq", "ch"), P(None, "seq"), P())
    return jax.shard_map(
        local,
        mesh=mesh,
        in_specs=placed,
        out_specs=(P("seq", "ch"), P(None, "seq")),
        check_vma=False,
    )
```

profile of v0, /device:TPU:1, one launch (start us, length us, event | category | flops | bytes accessed | tf_op | source)
XLA Modules:
  0.0 598.3 jit_solution(6543124483362616095)
XLA Ops:
  8.8 17.1 %all-to-all-start = ((bf16[64,8,128]{2,1,0:T(8,128)(2,1)}), bf16[64,8,128]{2,1,0:T(8,128)(2,1)S(1)}, u32[]{:S(2)}, u32[]{:S(2)}) async-start(bf16[64,8,128]{2,1,0:T(8,128)(2,1)} %bitcast.1), calls=%async_computation | async-start | bytes 262144 | tf_op jit(solution)/shard_map/all_to_all | solution.py:44
  26.0 37.6 %all_gather.3 = bf16[4,8192]{1,0:T(4,128)(2,1)S(1)} all-gather(bf16[4,128]{1,0:T(4,128)(2,1)} %param.14), channel_id=1, replica_groups=mesh['seq'=64,'ch'=8] {'seq'}, dimensions={1}, use_global_device_ids=true | all-gather | bytes 66560 | tf_op jit(solution)/shard_map/all_gather | solution.py:52
  67.6 8.9 %all-to-all-start.1 = ((bf16[64,8,128]{2,1,0:T(8,128)(2,1)}), bf16[64,8,128]{2,1,0:T(8,128)(2,1)S(1)}, u32[]{:S(2)}, u32[]{:S(2)}) async-start(bf16[64,8,128]{2,1,0:T(8,128)(2,1)} %bitcast.3), calls=%async_computation.1 | async-start | bytes 262144 | tf_op jit(solution)/shard_map/all_to_all | solution.py:45
  78.2 9.9 %all-to-all-done.1 = bf16[64,8,128]{2,1,0:T(8,128)(2,1)S(1)} async-done(((bf16[64,8,128]{2,1,0:T(8,128)(2,1)}), bf16[64,8,128]{2,1,0:T(8,128)(2,1)S(1)}, u32[]{:S(2)}, u32[]{:S(2)}) %all-to-all-start.1) | async-done | bytes 131104 | tf_op jit(solution)/shard_map/all_to_all | solution.py:45
  95.4 8.9 %reshape.208 = bf16[2179068]{0:T(1024)(128)(2,1)} reshape(bf16[4,129,4223]{2,1,0:T(8,128)(2,1)} %tile.20) | data formatting | bytes 8716272
  104.3 7.0 %tile.21 = bf16[4,544767]{1,0:T(4,128)(2,1)} reshape(bf16[2179068]{0:T(1024)(128)(2,1)} %reshape.208) | data formatting | bytes 8716272 | tf_op jit(solution)/shard_map/tile | solution.py:12
  111.4 7.0 %slice.342 = bf16[4,540416]{1,0:T(4,128)(2,1)} slice(bf16[4,544767]{1,0:T(4,128)(2,1)} %tile.21), slice={[0:4], [127:540543]} | slice | bytes 8646656 | tf_op jit(solution)/shard_map/slice | solution.py:14
  118.4 5.9 reshape.210
  124.3 11.5 %reshape.142 = bf16[4,128,4222]{2,1,0:T(8,128)(2,1)} reshape(bf16[2161664]{0:T(1024)(128)(2,1)} %reshape.210) | data formatting | bytes 8646656 | tf_op jit(solution)/shard_map/reshape | solution.py:15
  138.2 18.9 %reshape.204 = bf16[2179068]{0:T(1024)(128)(2,1)} reshape(bf16[4,129,4223]{2,1,0:T(8,128)(2,1)} %tile.8) | data formatting | bytes 8716272
  157.1 7.0 %tile.9 = bf16[4,544767]{1,0:T(4,128)(2,1)} reshape(bf16[2179068]{0:T(1024)(128)(2,1)} %reshape.204) | data formatting | bytes 8716272 | tf_op jit(solution)/shard_map/tile | solution.py:12
  164.2 6.8 %slice.338 = bf16[4,540416]{1,0:T(4,128)(2,1)} slice(bf16[4,544767]{1,0:T(4,128)(2,1)} %tile.9), slice={[0:4], [127:540543]} | slice | bytes 8646656 | tf_op jit(solution)/shard_map/slice | solution.py:14
  176.8 11.5 %reshape.141 = bf16[4,128,4222]{2,1,0:T(8,128)(2,1)} reshape(bf16[2161664]{0:T(1024)(128)(2,1)} %reshape.206) | data formatting | bytes 8646656 | tf_op jit(solution)/shard_map/reshape | solution.py:15
  209.3 12.5 %copy.48 = f32[1,4,128,4224]{3,1,2,0:T(4,128)} copy(f32[1,4,128,4224]{3,2,1,0:T(8,128)} %pad_bitcast_fusion.1) | data formatting | bytes 17301504
  221.8 8.6 %slice.344 = f32[4,540544]{1,0:T(4,128)} slice(f32[4,540672]{1,0:T(4,128)} %bitcast.82), slice={[0:4], [0:540544]} | slice | bytes 17297408 | tf_op jit(solution)/shard_map/slice | solution.py:24
  230.4 10.2 %reshape.212 = f32[2162176]{0:T(1024)} reshape(f32[4,540544]{1,0:T(4,128)} %slice.344) | data formatting | bytes 17297408
  240.6 13.1 %reshape.150 = f32[4,128,4223]{2,1,0:T(8,128)} reshape(f32[2162176]{0:T(1024)} %reshape.212) | data formatting | bytes 17297408 | tf_op jit(solution)/shard_map/reshape | solution.py:24
  263.9 12.3 %copy.49 = f32[1,4,128,4224]{3,1,2,0:T(4,128)} copy(f32[1,4,128,4224]{3,2,1,0:T(8,128)} %pad_bitcast_fusion) | data formatting | bytes 17301504
  276.2 8.6 %slice.346 = f32[4,540544]{1,0:T(4,128)} slice(f32[4,540672]{1,0:T(4,128)} %bitcast.83), slice={[0:4], [0:540544]} | slice | bytes 17297408 | tf_op jit(solution)/shard_map/slice | solution.py:24
  284.8 10.2 %reshape.214 = f32[2162176]{0:T(1024)} reshape(f32[4,540544]{1,0:T(4,128)} %slice.346) | data formatting | bytes 17297408
  295.0 13.1 %reshape.152 = f32[4,128,4223]{2,1,0:T(8,128)} reshape(f32[2162176]{0:T(1024)} %reshape.214) | data formatting | bytes 17297408 | tf_op jit(solution)/shard_map/reshape | solution.py:24
  316.1 23.5 %all_to_all.48 = bf16[8,64,128]{2,0,1:T(8,128)(2,1)S(1)} all-to-all(bf16[8,64,128]{2,0,1:T(8,128)(2,1)S(1)} %copy.33), channel_id=1, replica_groups=mesh['seq'=64,'ch'=8] {'seq'}, dimensions={1} | all-to-all | bytes 262144 | tf_op jit(solution)/shard_map/all_to_all | solution.py:109
  340.4 232.0 %reduce-scatter.4.cloned.1.call-done = f32[128,4]{1,0:T(8,128)} async-done(((f32[8192,4]{1,0:T(8,128)}), f32[128,4]{1,0:T(8,128)}) %reduce-scatter.4.cloned.1.call-update) | async-done | bytes 2064
  573.3 17.8 %psum.7 = f32[4,128]{1,0:T(4,128)} all-reduce(f32[4,128]{1,0:T(4,128)S(1)} %copy.47), channel_id=1, replica_groups=mesh['seq'=64,'ch'=8] {'ch'}, use_global_device_ids=true, to_apply=%region_5.7 | all-reduce | flops 512 | bytes 4096 | tf_op jit(solution)/shard_map/psum | solution.py:113
  (139 shorter events, 63.2 us)
Async XLA Ops:
  8.8 58.8 %all-to-all-start = ((bf16[64,8,128]{2,1,0:T(8,128)(2,1)}), bf16[64,8,128]{2,1,0:T(8,128)(2,1)S(1)}, u32[]{:S(2)}, u32[]{:S(2)}) async-start(bf16[64,8,128]{2,1,0:T(8,128)(2,1)} %bitcast.1), calls=%async_computation | async-start | bytes 262144 | tf_op jit(solution)/shard_map/all_to_all | solution.py:44
  67.6 20.4 %all-to-all-start.1 = ((bf16[64,8,128]{2,1,0:T(8,128)(2,1)}), bf16[64,8,128]{2,1,0:T(8,128)(2,1)S(1)}, u32[]{:S(2)}, u32[]{:S(2)}) async-start(bf16[64,8,128]{2,1,0:T(8,128)(2,1)} %bitcast.3), calls=%async_computation.1 | async-start | bytes 262144 | tf_op jit(solution)/shard_map/all_to_all | solution.py:45
  88.0 101.7 %all-to-all-start.3 = ((bf16[64,8,128]{2,1,0:T(8,128)(2,1)}), bf16[64,8,128]{2,1,0:T(8,128)(2,1)S(1)}, u32[]{:S(2)}, u32[]{:S(2)}) async-start(bf16[64,8,128]{2,1,0:T(8,128)(2,1)} %bitcast.19), calls=%async_computation.3 | async-start | bytes 262144 | tf_op jit(solution)/shard_map/all_to_all | solution.py:46
  92.7 479.7 %reduce-scatter.4.cloned.1.call-start = ((), (), s32[]{:S(2)}) async-start(), calls=%async_computation.5 | async-start | bytes 4259840
  192.4 3.4 slice-start
  193.4 6.8 %slice-start.2 = ((s8[4325376]{0:T(1024)(128)(4,1)}), s8[4194304]{0:T(1024)(128)(4,1)S(1)}, s32[]{:S(2)}) async-start(s8[4325376]{0:T(1024)(128)(4,1)} %bitcast.87), calls=%async_computation.8 | async-start | bytes 8388608
  194.3 4.3 slice-start.1
  194.8 5.3 copy-start
  195.4 4.8 slice-start.3
Sparse Core Ops, SparseCore 0:
  315.0 257.3 reduce-scatter.3
where the time goes:
time: 603 us; the launch traced here: 598 us
  waiting for transfers between devices  242 us (40%)
  local copies, waits for them, and re-layouts  212 us (35%)
  blocking collectives  78.8 us (13%)
  starting transfers between devices  30.9 us (5%)
  between operations  15.2 us (3%)
  other arithmetic  11.6 us (2%)
  matrix products  7.54 us (1%)
    unnamed x2, waiting for transfers between devices  232 us
    unnamed x87, local copies, waits for them, and re-layouts  108 us
    all_gather x1, blocking collectives, local(): whole_taps = lax.all_gather(filter_taps, 'seq', axis=1, tiled=True)  37.6 us
    reshape x2, local copies, waits for them, and re-layouts, skewed_sums(): flat_part[..., :row_count * (col_count + row_count - 1)]  26.1 us
    all_to_all x1, blocking collectives, local(): lax.all_to_all(slot_cols, 'seq', split_axis=1, concat_axis=0, tiled=True)  23.5 us
    reshape x2, local copies, waits for them, and re-layouts, toeplitz_panel(): flat_part.reshape(leading + (row_count, seg_len - 1))[..., :col_count]  23 us
    another operation x4, local copies, waits for them, and re-layouts, toeplitz_panel(): repeated = jnp.tile(segment, (1,) * len(leading) + (row_count + 1,))  19 us
    psum x1, blocking collectives, local(): filter_grad = lax.psum(reduced, 'ch')  17.8 us
  transfers between devices with their start and end apart: 4, of which 2 were waited for; matrix products, arithmetic and copies ran while one was open for 17% of the time, Pallas kernels for 0%

commit v1 on v0

v1 whole, which is shorter than its diff:
```python
import functools
import math

import jax
import jax.numpy as jnp
from jax import lax
from jax.experimental import pallas as pl
from jax.experimental.pallas import tpu as pltpu
from jax.sharding import PartitionSpec as P

MESH = pl.DeviceIdType.MESH
LANES = 128
HALF = 64
SPAN = 8


def kernel(
    seq_count,
    ch_count,
    up_ref,
    gate_ref,
    value_ref,
    taps_ref,
    ids_ref,
    vg_ref,
    fg_ref,
    row_taps,
    all_taps,
    send1,
    recv1,
    wide1,
    grad_rows,
    value_rows,
    toeplitz,
    hankel,
    lag_mat,
    out_rows,
    wide2,
    send2,
    recv2,
    part,
    parts,
    send_sems,
    recv_sems,
):
    f32, bf16 = jnp.float32, jnp.bfloat16
    y_count = 1 << ((seq_count.bit_length() - 1) // 2)
    z_count = seq_count // y_count
    me = lax.axis_index("seq")
    my_ch = lax.axis_index("ch")
    my_z, my_y = lax.div(me, y_count), lax.rem(me, y_count)
    blocks = seq_count
    live = 2 * blocks
    panels = blocks // SPAN
    norm_scale = 1.0 / math.sqrt(blocks * LANES)

    def partner(d):
        z = lax.rem(my_z + lax.div(d, y_count), z_count)
        y = lax.rem(my_y + lax.rem(d, y_count), y_count)
        return z * y_count + y

    barrier = pltpu.get_barrier_semaphore()

    def greet(d, carry):
        pl.semaphore_signal(barrier, inc=1, device_id={"seq": partner(d)}, device_id_type=MESH)
        return carry

    lax.fori_loop(1, seq_count, greet, 0)

    def greet_ch(d, carry):
        pl.semaphore_signal(
            barrier, inc=1, device_id={"ch": lax.rem(my_ch + d, ch_count)}, device_id_type=MESH
        )
        return carry

    lax.fori_loop(1, ch_count, greet_ch, 0)

    row_id = lax.broadcasted_iota(jnp.int32, (LANES, LANES), 0)
    lane_id = lax.broadcasted_iota(jnp.int32, (LANES, LANES), 1)
    flip = (row_id + lane_id == LANES - 1).astype(bf16)
    row_taps[my_y] = jnp.dot(taps_ref[...], flip, preferred_element_type=f32)

    for c in range(up_ref.shape[1] // LANES):
        cols = pl.ds(c * LANES, LANES)
        product = up_ref[:, cols].astype(f32) * gate_ref[:, cols].astype(f32)
        value = value_ref[:, cols].astype(f32)
        group = LANES // 8
        send1[pl.ds(c * group, group)] = jnp.concatenate(
            [
                product.T.reshape(group, 8, LANES),
                value.T.reshape(group, 8, LANES),
            ],
            axis=1,
        ).astype(bf16)

    pl.semaphore_wait(barrier, seq_count - 1 + ch_count - 1)

    def send_y(d, carry):
        to = my_z * y_count + lax.rem(my_y + d, y_count)
        pltpu.make_async_remote_copy(
            src_ref=row_taps.at[my_y],
            dst_ref=row_taps.at[my_y],
            send_sem=send_sems.at[0],
            recv_sem=recv_sems.at[0],
            device_id={"seq": to},
            device_id_type=MESH,
        ).start()
        return carry

    lax.fori_loop(1, y_count, send_y, 0)

    def send_first(d, carry):
        to = partner(d)
        pltpu.make_async_remote_copy(
            src_ref=send1.at[to],
            dst_ref=recv1.at[me],
            send_sem=send_sems.at[1],
            recv_sem=recv_sems.at[1],
            device_id={"seq": to},
            device_id_type=MESH,
        ).start()
        return carry

    lax.fori_loop(1, seq_count, send_first, 0)
    recv1[me] = send1[me]

    def wait_all(ref, sem):
        pltpu.make_async_copy(ref, ref, sem).wait()

    wait_all(row_taps.at[pl.ds(0, y_count - 1)], recv_sems.at[0])

    def send_z(d, carry):
        to = lax.rem(my_z + d, z_count) * y_count + my_y
        pltpu.make_async_remote_copy(
            src_ref=row_taps,
            dst_ref=all_taps.at[pl.ds(my_z * y_count, y_count)],
            send_sem=send_sems.at[2],
            recv_sem=recv_sems.at[2],
            device_id={"seq": to},
            device_id_type=MESH,
        ).start()
        return carry

    lax.fori_loop(1, z_count, send_z, 0)
    all_taps[pl.ds(my_z * y_count, y_count)] = row_taps[...]
    wait_all(all_taps.at[pl.ds(0, (z_count - 1) * y_count)], recv_sems.at[2])

    filters = taps_ref.shape[0]
    for f in range(filters):

        def build(o, before):
            row = jnp.broadcast_to(all_taps[o, f : f + 1, :], (LANES, LANES))
            now = pltpu.roll(row, 1, 1, stride=1, stride_axis=0)
            block = jnp.where(lane_id > row_id, before, now)
            toeplitz[f, pl.ds(pl.multiple_of(o * LANES, LANES), LANES), :] = block.astype(bf16)
            return now

        lax.fori_loop(0, blocks, build, jnp.zeros((LANES, LANES), f32))

    wait_all(recv1.at[pl.ds(0, seq_count - 1)], recv_sems.at[1])

    halves = 2 * blocks
    slot = lax.broadcasted_iota(jnp.int32, (halves, halves), 0)
    column = lax.broadcasted_iota(jnp.int32, (halves, halves), 1)
    split = (2 * lax.rem(column, blocks) + lax.div(column, blocks) == slot).astype(bf16)
    ids = ids_ref[...].reshape(1, halves).astype(f32).astype(bf16)
    split_ids = jnp.dot(ids, split, preferred_element_type=f32).astype(jnp.int32)
    half = 2 * lax.rem(slot, blocks) + lax.div(slot, blocks)
    place = jnp.where(half == split_ids, 1.0, 0.0)

    low_lane = lax.broadcasted_iota(jnp.int32, (blocks, LANES), 1) < HALF

    def doubled(rows):
        other = pltpu.roll(rows, HALF, 1)
        return jnp.concatenate(
            [jnp.where(low_lane, rows, other), jnp.where(low_lane, other, rows)], axis=0
        ).astype(bf16)

    def joined(rows):
        return jnp.where(low_lane, rows[0:blocks], rows[blocks : 2 * blocks])

    wide1[...] = recv1[...].astype(f32).reshape(blocks * 16, LANES)
    sorter = place.astype(bf16)
    for c in range(16):
        rows = doubled(wide1[pl.ds(c, blocks, stride=16), :])
        rows = joined(jnp.dot(sorter, rows, preferred_element_type=f32))
        a, f = (c % 8) // filters, c % filters
        target = grad_rows if c < 8 else value_rows
        target[f, pl.ds(a, blocks, stride=2), :] = rows
    for f in range(filters):
        grad_rows[f, pl.ds(live, 2 * SPAN), :] = jnp.zeros((2 * SPAN, LANES), f32)

    for f in range(filters):
        for o in range(SPAN):
            hankel[f, pl.ds(0, live), pl.ds(o * LANES, LANES)] = grad_rows[
                f, pl.ds(2 * o, live), :
            ].astype(bf16)
        hankel[f, pl.ds(live, live), :] = jnp.zeros((live, SPAN * LANES), bf16)

        turned = lax.dot_general(
            flip,
            value_rows[f].astype(bf16),
            (((1,), (1,)), ((), ())),
            preferred_element_type=f32,
        ).astype(bf16)

        def contract(p, total):
            rows = pl.ds(pl.multiple_of(p * 2 * SPAN, 2 * SPAN), live)
            wide = pl.ds(pl.multiple_of(p * SPAN * LANES, SPAN * LANES), SPAN * LANES)
            panel = hankel[f, rows, :]
            lag_mat[:, wide] = jnp.dot(turned, panel, preferred_element_type=f32)
            return total + jnp.dot(panel, toeplitz[f, wide, :], preferred_element_type=f32)

        total = lax.fori_loop(0, panels, contract, jnp.zeros((live, LANES), f32))
        out_rows[f] = total * norm_scale
        lag_mat[:, pl.ds(blocks * LANES, LANES)] = jnp.zeros((LANES, LANES), f32)

        def skew(o, carry):
            here = lag_mat[:, pl.ds(pl.multiple_of(o * LANES, LANES), LANES)]
            after = lag_mat[:, pl.ds(pl.multiple_of((o + 1) * LANES, LANES), LANES)]
            chosen = jnp.where(row_id + lane_id >= LANES - 1, here, after)
            rolled = pltpu.roll(chosen, 1, 1, stride=1, stride_axis=0)
            row = jnp.sum(rolled, axis=0, keepdims=True) * norm_scale
            rounded = row.astype(bf16).astype(f32)
            wide2[pl.ds(o * 16 + 8 + f, 1), :] = rounded
            wide2[pl.ds(o * 16 + 12 + f, 1), :] = row - rounded
            return carry

        lax.fori_loop(0, blocks, skew, 0)

    unsorter = place.T.astype(bf16)
    for c in range(8):
        rows = doubled(out_rows[c % filters, pl.ds(c // filters, blocks, stride=2), :])
        rows = joined(jnp.dot(unsorter, rows, preferred_element_type=f32))
        wide2[pl.ds(c, blocks, stride=16), :] = rows
    send2[...] = wide2[...].reshape(blocks, 16, LANES).astype(bf16)

    def send_back(d, carry):
        to = partner(d)
        pltpu.make_async_remote_copy(
            src_ref=send2.at[to],
            dst_ref=recv2.at[me],
            send_sem=send_sems.at[3],
            recv_sem=recv_sems.at[3],
            device_id={"seq": to},
            device_id_type=MESH,
        ).start()
        return carry

    lax.fori_loop(1, seq_count, send_back, 0)
    recv2[me] = send2[me]
    wait_all(recv2.at[pl.ds(0, seq_count - 1)], recv_sems.at[3])

    def add_lags(p, total):
        return total + recv2[p].astype(f32)

    summed = lax.fori_loop(0, seq_count, add_lags, jnp.zeros((16, LANES), f32))
    part[...] = summed[8:16]

    def send_ch(d, carry):
        pltpu.make_async_remote_copy(
            src_ref=part,
            dst_ref=parts.at[my_ch],
            send_sem=send_sems.at[4],
            recv_sem=recv_sems.at[4],
            device_id={"ch": lax.rem(my_ch + d, ch_count)},
            device_id_type=MESH,
        ).start()
        return carry

    lax.fori_loop(1, ch_count, send_ch, 0)
    parts[my_ch] = part[...]

    for c in range(vg_ref.shape[1] // LANES):
        group = LANES // 8
        rows = recv2[pl.ds(c * group, group)].astype(f32)[:, 0:8, :].reshape(LANES, LANES)
        vg_ref[:, pl.ds(c * LANES, LANES)] = rows.T.astype(bf16)

    wait_all(parts.at[pl.ds(0, ch_count - 1)], recv_sems.at[4])
    both = jnp.sum(parts[...], axis=0)
    fg_ref[...] = both[0:filters] + both[filters : 2 * filters]

    wait_all(row_taps.at[pl.ds(0, y_count - 1)], send_sems.at[0])
    wait_all(send1.at[pl.ds(0, seq_count - 1)], send_sems.at[1])
    wait_all(all_taps.at[pl.ds(0, (z_count - 1) * y_count)], send_sems.at[2])
    wait_all(send2.at[pl.ds(0, seq_count - 1)], send_sems.at[3])
    wait_all(parts.at[pl.ds(0, ch_count - 1)], send_sems.at[4])


def local(upstream_grad, gate_act, value_act, filter_taps, half_ids):
    seq_count = lax.axis_size("seq")
    ch_count = lax.axis_size("ch")
    local_rows, channels = upstream_grad.shape
    filters = filter_taps.shape[0]
    blocks = seq_count
    y_count = 1 << ((seq_count.bit_length() - 1) // 2)
    f32, bf16 = jnp.float32, jnp.bfloat16
    vmem = pl.BlockSpec(memory_space=pltpu.VMEM)
    return pl.pallas_call(
        functools.partial(kernel, seq_count, ch_count),
        out_shape=(
            jax.ShapeDtypeStruct((local_rows, channels), bf16),
            jax.ShapeDtypeStruct((filters, LANES), f32),
        ),
        in_specs=[vmem] * 5,
        out_specs=(vmem, vmem),
        scratch_shapes=[
            pltpu.VMEM((y_count, filters, LANES), f32),
            pltpu.VMEM((blocks, filters, LANES), f32),
            pltpu.VMEM((seq_count, 16, LANES), bf16),
            pltpu.VMEM((seq_count, 16, LANES), bf16),
            pltpu.VMEM((blocks * 16, LANES), f32),
            pltpu.VMEM((filters, 2 * (blocks + SPAN), LANES), f32),
            pltpu.VMEM((filters, 2 * blocks, LANES), f32),
            pltpu.VMEM((filters, blocks * LANES, LANES), bf16),
            pltpu.VMEM((filters, 4 * blocks, SPAN * LANES), bf16),
            pltpu.VMEM((LANES, (blocks + 1) * LANES), f32),
            pltpu.VMEM((filters, 2 * blocks, LANES), f32),
            pltpu.VMEM((blocks * 16, LANES), f32),
            pltpu.VMEM((seq_count, 16, LANES), bf16),
            pltpu.VMEM((seq_count, 16, LANES), bf16),
            pltpu.VMEM((8, LANES), f32),
            pltpu.VMEM((ch_count, 8, LANES), f32),
            pltpu.SemaphoreType.DMA((5,)),
            pltpu.SemaphoreType.DMA((5,)),
        ],
        compiler_params=pltpu.CompilerParams(
            collective_id=0, has_side_effects=True, vmem_limit_bytes=40 * 1024 * 1024
        ),
        cost_estimate=pl.CostEstimate(
            flops=4 * 8 * (blocks * LANES) ** 2,
            bytes_accessed=4 * local_rows * channels * 2,
            transcendentals=0,
        ),
    )(upstream_grad, gate_act, value_act, filter_taps, half_ids)


def solution(mesh):
    placed = (P("seq", "ch"), P("seq", "ch"), P("seq", "ch"), P(None, "seq"), P())
    return jax.shard_map(
        local,
        mesh=mesh,
        in_specs=placed,
        out_specs=(P("seq", "ch"), P(None, "seq")),
        check_vma=False,
    )
```

time: 603 us -> 108 us (0.18)
  waiting for transfers between devices: 242 us -> 0 us
  local copies, waits for them, and re-layouts: 212 us -> 5.27 us
  Pallas kernels: 0 us -> 102 us
  blocking collectives: 78.8 us -> 0 us
  starting transfers between devices: 30.9 us -> 0 us
  between operations: 15.2 us -> 0.65 us
  other arithmetic: 11.6 us -> 0 us
  matrix products: 7.54 us -> 0 us
    unnamed x2 -> x0, waiting for transfers between devices: 232 us -> none
    unnamed x87 -> x12, local copies, waits for them, and re-layouts: 108 us -> 5.27 us
    pallas_call x0 -> x1, Pallas kernels: none -> 102 us  [local(): pl.pallas_call(functools.partial(kernel, seq_count, ch_count), out_shape=...]
    reshape x14 -> x0, local copies, waits for them, and re-layouts: 50.5 us -> none  [the longest x2 26.1 us: skewed_sums(): flat_part[..., :row_count * (col_count + row_count - 1)]]
    all_gather x1 -> x0, blocking collectives: 37.6 us -> none  [local(): whole_taps = lax.all_gather(filter_taps, 'seq', axis=1, tiled=True)]
    slice x7 -> x0, local copies, waits for them, and re-layouts: 31.2 us -> none  [the longest x2 17.2 us: skewed_sums(): flat_part[..., :row_count * (col_count + row_count - 1)]]
    all_to_all x3 -> x0, starting transfers between devices: 30.6 us -> none  [the longest x1 17.1 us: local(): lax.all_to_all(to_columns(upstream_grad), 'seq', split_axis=0, concat_axi...]
    all_to_all x1 -> x0, blocking collectives: 23.5 us -> none  [local(): lax.all_to_all(slot_cols, 'seq', split_axis=1, concat_axis=0, tiled=True)]
  transfers between devices with their start and end apart: 4 -> 0, of which waited for: 2 -> 0; matrix products, arithmetic and copies ran while one was open for 17% -> 0% of each run, Pallas kernels for 0% -> 0%
where the time goes in v1:
time: 108 us
  Pallas kernels  102 us (94%)
  local copies, waits for them, and re-layouts  5.27 us (5%)
    pallas_call x1, Pallas kernels, local(): pl.pallas_call(functools.partial(kernel, seq_count, ch_count), out_shape=...  102 us
    unnamed x12, local copies, waits for them, and re-layouts  5.27 us

profile of v1, /device:TPU:1, one launch (start us, length us, event | category | flops | bytes accessed | tf_op | source)
XLA Modules:
  0.0 108.3 jit_solution(3478747425258508942)
XLA Ops:
  0.6 0.0 copy-start
  0.6 0.9 copy-done
  1.5 0.0 copy-start.1
  1.5 0.9 copy-done.1
  2.4 0.0 copy-start.2
  2.4 0.9 copy-done.2
  3.3 0.0 copy-start.3
  3.3 0.7 copy-done.3
  4.0 0.0 copy-start.4
  4.0 0.7 copy-done.4
  4.7 102.4 %shard_map.68 = (bf16[128,512]{1,0:T(8,128)(2,1)S(1)}, f32[4,128]{1,0:T(4,128)S(1)}) custom-call(bf16[128,512]{1,0:T(8,128)(2,1)S(1)} %copy-done, bf16[128,512]{1,0:T(8,128)(2,1)S(1)} %copy-done.1, bf16[128,512]{1,0:T(8,128)(2,1)S(1)} %copy-done.2, bf16[4,128]{1,0:T(4,128)(2,1)S(1)} %copy-done.3, s32[128]{0:T(128)S(1)} %copy-done.4), custom_call_target="tpu_custom_call" | custom-call | flops 2147483648 | bytes 524288 | tf_op jit(solution)/shard_map/pallas_call | solution.py:299
  107.1 0.7 copy.9
  107.7 0.6 copy.10
Async XLA Ops:
  0.6 0.9 copy-start
  1.5 0.9 copy-start.1
  2.4 0.9 copy-start.2
  3.3 0.7 copy-start.3
  4.0 0.7 copy-start.4

commit v2 on v1

v2 whole, which is shorter than its diff:
```python
import functools
import math

import jax
import jax.numpy as jnp
import ml_dtypes
import numpy as np
from jax import lax
from jax.experimental import pallas as pl
from jax.experimental.pallas import tpu as pltpu
from jax.sharding import PartitionSpec as P

MESH = pl.DeviceIdType.MESH
LANES = 128
HALF = 64


def two_parts(table):
    high = table.astype(ml_dtypes.bfloat16)
    rest = (table - high.astype(np.float64)).astype(ml_dtypes.bfloat16)
    return high, rest


@functools.lru_cache(maxsize=None)
def tables(halves):
    tall = 2 * halves
    points = tall * HALF
    angle = 2 * np.pi * np.outer(np.arange(tall), np.arange(halves)) / tall
    cosine, sine = np.cos(angle), -np.sin(angle)
    parts = two_parts(cosine) + two_parts(sine)
    forward = np.concatenate(parts, 0)
    back = np.ascontiguousarray(np.concatenate(parts, 0).T)
    natural = np.concatenate([np.arange(0, halves, 2), np.arange(1, halves, 2)])
    both = np.concatenate([cosine, sine], 0)[:, natural]
    taps = np.concatenate(two_parts(both), 1)
    lags = np.stack(two_parts(np.ascontiguousarray(both.T)))
    turn = 2 * np.pi * np.outer(np.arange(tall), np.arange(HALF)) / points
    turn = np.tile(turn, (1, 2))
    twiddle = np.stack([np.cos(turn), -np.sin(turn)]).astype(np.float32)
    small = 2 * np.pi * np.outer(np.arange(HALF), np.arange(HALF)) / HALF
    pair = np.eye(2)
    real, imag = np.kron(pair, np.cos(small)), np.kron(pair, -np.sin(small))
    inner = np.stack(two_parts(np.block([[real, imag], [-imag, real]])))
    outer = np.stack(two_parts(np.block([[real, -imag], [imag, real]])))
    return forward, back, taps, lags, twiddle, inner, outer


def kernel(
    seq_count,
    ch_count,
    up_hbm,
    gate_hbm,
    value_hbm,
    taps_hbm,
    ids_hbm,
    forward_hbm,
    back_hbm,
    taps_tab_hbm,
    lags_hbm,
    twiddle_hbm,
    inner_hbm,
    outer_hbm,
    vg_ref,
    fg_ref,
    up_ref,
    gate_ref,
    value_ref,
    taps_ref,
    ids_ref,
    forward,
    back,
    taps_tab,
    lags_tab,
    twiddle,
    inner,
    outer,
    row_taps,
    packed_taps,
    all_taps,
    send1,
    recv1,
    wide1,
    left,
    left_back,
    spectra,
    wide2,
    send2,
    recv2,
    part,
    parts,
    load_sems,
    send_sems,
    recv_sems,
):
    f32, bf16 = jnp.float32, jnp.bfloat16
    y_count = 1 << ((seq_count.bit_length() - 1) // 2)
    z_count = seq_count // y_count
    me = lax.axis_index("seq")
    my_ch = lax.axis_index("ch")
    my_z, my_y = lax.div(me, y_count), lax.rem(me, y_count)
    blocks = seq_count
    halves = 2 * blocks
    tall = 2 * halves
    filters = taps_ref.shape[0]
    scale = 1.0 / math.sqrt(blocks * LANES) / (tall * HALF)

    pairs = (
        (up_hbm, up_ref),
        (gate_hbm, gate_ref),
        (value_hbm, value_ref),
        (taps_hbm, taps_ref),
        (ids_hbm, ids_ref),
        (forward_hbm, forward),
        (back_hbm, back),
        (taps_tab_hbm, taps_tab),
        (lags_hbm, lags_tab),
        (twiddle_hbm, twiddle),
        (inner_hbm, inner),
        (outer_hbm, outer),
    )
    loads = [
        pltpu.make_async_copy(src, dst, load_sems.at[i]) for i, (src, dst) in enumerate(pairs)
    ]
    for load in loads:
        load.start()

    def partner(d):
        z = lax.rem(my_z + lax.div(d, y_count), z_count)
        y = lax.rem(my_y + lax.rem(d, y_count), y_count)
        return z * y_count + y

    barrier = pltpu.get_barrier_semaphore()

    def greet(d, carry):
        pl.semaphore_signal(barrier, inc=1, device_id={"seq": partner(d)}, device_id_type=MESH)
        return carry

    lax.fori_loop(1, seq_count, greet, 0)

    def greet_ch(d, carry):
        pl.semaphore_signal(
            barrier, inc=1, device_id={"ch": lax.rem(my_ch + d, ch_count)}, device_id_type=MESH
        )
        return carry

    lax.fori_loop(1, ch_count, greet_ch, 0)

    for load in loads[0:4]:
        load.wait()
    own = taps_ref[...].astype(f32)
    row_taps[pl.ds(pl.multiple_of(my_y * 8, 8), 8), :] = jnp.concatenate([own, own], axis=0)

    group = LANES // 8
    for c in range(up_ref.shape[1] // LANES):
        cols = pl.ds(c * LANES, LANES)
        product = up_ref[:, cols].astype(f32) * gate_ref[:, cols].astype(f32)
        value = value_ref[:, cols].astype(f32)
        send1[pl.ds(c * group, group)] = jnp.concatenate(
            [product.T.reshape(group, 8, LANES), value.T.reshape(group, 8, LANES)], axis=1
        ).astype(bf16)

    pl.semaphore_wait(barrier, seq_count - 1 + ch_count - 1)

    def send_y(d, carry):
        mine = row_taps.at[pl.ds(pl.multiple_of(my_y * 8, 8), 8)]
        pltpu.make_async_remote_copy(
            src_ref=mine,
            dst_ref=mine,
            send_sem=send_sems.at[0],
            recv_sem=recv_sems.at[0],
            device_id={"seq": my_z * y_count + lax.rem(my_y + d, y_count)},
            device_id_type=MESH,
        ).start()
        return carry

    lax.fori_loop(1, y_count, send_y, 0)

    def send_first(d, carry):
        to = partner(d)
        pltpu.make_async_remote_copy(
            src_ref=send1.at[to],
            dst_ref=recv1.at[me],
            send_sem=send_sems.at[1],
            recv_sem=recv_sems.at[1],
            device_id={"seq": to},
            device_id_type=MESH,
        ).start()
        return carry

    lax.fori_loop(1, seq_count, send_first, 0)
    recv1[me] = send1[me]

    def wait_all(ref, sem):
        pltpu.make_async_copy(ref, ref, sem).wait()

    wait_all(row_taps.at[pl.ds(0, (y_count - 1) * 8)], recv_sems.at[0])

    packed_taps[...] = jnp.concatenate(
        [row_taps[pl.ds(f, y_count, stride=8), :] for f in range(filters)], axis=0
    ).astype(bf16)

    def send_z(d, carry):
        pltpu.make_async_remote_copy(
            src_ref=packed_taps,
            dst_ref=all_taps.at[my_z],
            send_sem=send_sems.at[2],
            recv_sem=recv_sems.at[2],
            device_id={"seq": lax.rem(my_z + d, z_count) * y_count + my_y},
            device_id_type=MESH,
        ).start()
        return carry

    lax.fori_loop(1, z_count, send_z, 0)
    all_taps[my_z] = packed_taps[...]

    for load in loads[4:]:
        load.wait()
    slot = lax.broadcasted_iota(jnp.int32, (halves, halves), 0)
    column = lax.broadcasted_iota(jnp.int32, (halves, halves), 1)
    split = (2 * lax.rem(column, blocks) + lax.div(column, blocks) == slot).astype(bf16)
    ids = ids_ref[...].reshape(1, halves).astype(f32).astype(bf16)
    split_ids = jnp.dot(ids, split, preferred_element_type=f32).astype(jnp.int32)
    place = jnp.where(slot == split_ids, 1.0, 0.0)
    sorted_cols = jnp.dot(forward[...], place.astype(bf16), preferred_element_type=f32)
    sorted_rows = jnp.dot(place.T.astype(bf16), back[...], preferred_element_type=f32)
    for n in range(2):
        cosine, sine = sorted_cols[n * tall : (n + 1) * tall], sorted_cols[(n + 2) * tall : (n + 3) * tall]
        left[0:tall, n * tall : (n + 1) * tall] = jnp.concatenate([cosine, -sine], axis=1).astype(bf16)
        left[tall : 2 * tall, n * tall : (n + 1) * tall] = jnp.concatenate([sine, cosine], axis=1).astype(
            bf16
        )
        cosine = sorted_rows[:, n * tall : (n + 1) * tall]
        sine = sorted_rows[:, (n + 2) * tall : (n + 3) * tall]
        left_back[n, 0:halves, :] = jnp.concatenate([cosine, sine], axis=1).astype(bf16)
        left_back[n, halves : 2 * halves, :] = jnp.concatenate([-sine, cosine], axis=1).astype(bf16)

    low_lane = lax.broadcasted_iota(jnp.int32, (blocks, LANES), 1) < HALF

    def by_halves(rows0, rows1):
        return jnp.concatenate(
            [
                jnp.where(low_lane, rows0, pltpu.roll(rows1, HALF, 1)),
                jnp.where(low_lane, pltpu.roll(rows0, HALF, 1), rows1),
            ],
            axis=0,
        )

    def joined(rows):
        even, odd = rows[0:blocks], rows[blocks : 2 * blocks]
        return (
            jnp.where(low_lane, even, pltpu.roll(odd, HALF, 1)),
            jnp.where(low_lane, pltpu.roll(even, HALF, 1), odd),
        )

    def parts_of(x):
        high = x.astype(bf16)
        return high, (x - high.astype(f32)).astype(bf16)

    def dot(a, b):
        return jnp.dot(a, b, preferred_element_type=f32)

    def product_right(x, table):
        high, rest = parts_of(x)
        return dot(high, table[0]) + dot(high, table[1]) + dot(rest, table[0])

    def product_left(table, x):
        high, rest = parts_of(x)
        return dot(table[0], high) + dot(table[1], high) + dot(table[0], rest)

    def spectrum(re, im):
        cosine, sine = twiddle[0], twiddle[1]
        turned = jnp.concatenate([re * cosine - im * sine, re * sine + im * cosine], axis=1)
        return product_right(turned, inner)

    def conj_times(a, b):
        ar, ai = a[:, 0:LANES], a[:, LANES:]
        br, bi = b[:, 0:LANES], b[:, LANES:]
        return jnp.concatenate([ar * br + ai * bi, ar * bi - ai * br], axis=1)

    def unturned(x):
        y = product_right(x, outer)
        re, im = y[:, 0:LANES], y[:, LANES:]
        cosine, sine = twiddle[0], twiddle[1]
        return jnp.concatenate([re * cosine + im * sine, im * cosine - re * sine], axis=0)

    wait_all(all_taps.at[pl.ds(0, z_count - 1)], recv_sems.at[2])
    taps_wide = all_taps[...].astype(f32)

    def taps_of(f):
        return taps_wide[:, f * y_count : (f + 1) * y_count, :].reshape(blocks, LANES)

    taps_in = jnp.concatenate(
        [by_halves(taps_of(f), taps_of(f + 1)) for f in range(0, filters, 2)], axis=1
    ).astype(bf16)
    taps_first = dot(taps_tab[...], jnp.concatenate([taps_in, taps_in], axis=0))
    for q in range(filters // 2):
        lanes = slice(q * LANES, (q + 1) * LANES)
        spectra[q] = spectrum(taps_first[0:tall, lanes], taps_first[tall:, lanes])

    wait_all(recv1.at[pl.ds(0, seq_count - 1)], recv_sems.at[1])
    wide1[...] = recv1[...].astype(f32).reshape(blocks * 16, LANES)

    def first_stage(base):
        columns = []
        for f in range(0, filters, 2):
            rows = [
                by_halves(
                    wide1[pl.ds(base + a * filters + f, blocks, stride=16), :],
                    wide1[pl.ds(base + a * filters + f + 1, blocks, stride=16), :],
                )
                for a in range(2)
            ]
            columns.append(jnp.concatenate(rows, axis=0))
        data = jnp.concatenate(columns, axis=1).astype(bf16)
        return dot(left[...], jnp.concatenate([data, data], axis=0))

    grad_first = first_stage(0)
    value_first = first_stage(8)
    grad_back, lag_back = [], []
    for q in range(filters // 2):
        lanes = slice(q * LANES, (q + 1) * LANES)
        grad_spec = spectrum(grad_first[0:tall, lanes], grad_first[tall:, lanes])
        value_spec = spectrum(value_first[0:tall, lanes], value_first[tall:, lanes])
        grad_back.append(unturned(conj_times(spectra[q], grad_spec)))
        lag_back.append(unturned(conj_times(value_spec, grad_spec)))
    in_grad = product_left(left_back, jnp.concatenate(grad_back, axis=1)) * scale
    lag_sums = product_left(lags_tab, jnp.concatenate(lag_back, axis=1)) * scale

    for q in range(filters // 2):
        lanes = slice(q * LANES, (q + 1) * LANES)
        for a in range(2):
            for n, rows in enumerate(joined(in_grad[a * halves : (a + 1) * halves, lanes])):
                wide2[pl.ds(a * filters + 2 * q + n, blocks, stride=16), :] = rows
        for n, rows in enumerate(joined(lag_sums[:, lanes])):
            rounded = rows.astype(bf16).astype(f32)
            wide2[pl.ds(8 + 2 * q + n, blocks, stride=16), :] = rounded
            wide2[pl.ds(8 + filters + 2 * q + n, blocks, stride=16), :] = rows - rounded
    send2[...] = wide2[...].reshape(blocks, 16, LANES).astype(bf16)

    def send_back(d, carry):
        to = partner(d)
        pltpu.make_async_remote_copy(
            src_ref=send2.at[to],
            dst_ref=recv2.at[me],
            send_sem=send_sems.at[3],
            recv_sem=recv_sems.at[3],
            device_id={"seq": to},
            device_id_type=MESH,
        ).start()
        return carry

    lax.fori_loop(1, seq_count, send_back, 0)
    recv2[me] = send2[me]
    wait_all(recv2.at[pl.ds(0, seq_count - 1)], recv_sems.at[3])

    def add_lags(p, total):
        return total + recv2[p].astype(f32)

    summed = lax.fori_loop(0, seq_count, add_lags, jnp.zeros((16, LANES), f32))
    part[...] = summed[8:16]

    def send_ch(d, carry):
        pltpu.make_async_remote_copy(
            src_ref=part,
            dst_ref=parts.at[my_ch],
            send_sem=send_sems.at[4],
            recv_sem=recv_sems.at[4],
            device_id={"ch": lax.rem(my_ch + d, ch_count)},
            device_id_type=MESH,
        ).start()
        return carry

    lax.fori_loop(1, ch_count, send_ch, 0)
    parts[my_ch] = part[...]

    for c in range(vg_ref.shape[1] // LANES):
        rows = recv2[pl.ds(c * group, group)].astype(f32)[:, 0:8, :].reshape(LANES, LANES)
        vg_ref[:, pl.ds(c * LANES, LANES)] = rows.T.astype(bf16)

    wait_all(parts.at[pl.ds(0, ch_count - 1)], recv_sems.at[4])
    both = jnp.sum(parts[...], axis=0)
    fg_ref[...] = both[0:filters] + both[filters : 2 * filters]

    wait_all(row_taps.at[pl.ds(0, (y_count - 1) * 8)], send_sems.at[0])
    wait_all(send1.at[pl.ds(0, seq_count - 1)], send_sems.at[1])
    wait_all(all_taps.at[pl.ds(0, z_count - 1)], send_sems.at[2])
    wait_all(send2.at[pl.ds(0, seq_count - 1)], send_sems.at[3])
    wait_all(parts.at[pl.ds(0, ch_count - 1)], send_sems.at[4])


def local(upstream_grad, gate_act, value_act, filter_taps, half_ids):
    seq_count = lax.axis_size("seq")
    ch_count = lax.axis_size("ch")
    local_rows, channels = upstream_grad.shape
    filters = filter_taps.shape[0]
    blocks = seq_count
    halves = 2 * blocks
    tall = 2 * halves
    y_count = 1 << ((seq_count.bit_length() - 1) // 2)
    f32, bf16 = jnp.float32, jnp.bfloat16
    constants = [jnp.asarray(table) for table in tables(halves)]
    vmem = pl.BlockSpec(memory_space=pltpu.VMEM)
    operands = [upstream_grad, gate_act, value_act, filter_taps, half_ids] + constants
    return pl.pallas_call(
        functools.partial(kernel, seq_count, ch_count),
        out_shape=(
            jax.ShapeDtypeStruct((local_rows, channels), bf16),
            jax.ShapeDtypeStruct((filters, LANES), f32),
        ),
        in_specs=[pl.BlockSpec(memory_space=pl.ANY)] * len(operands),
        out_specs=(vmem, vmem),
        scratch_shapes=[pltpu.VMEM(x.shape, x.dtype) for x in operands]
        + [
            pltpu.VMEM((y_count * 8, LANES), f32),
            pltpu.VMEM((filters * y_count, LANES), bf16),
            pltpu.VMEM((seq_count // y_count, filters * y_count, LANES), bf16),
            pltpu.VMEM((seq_count, 16, LANES), bf16),
            pltpu.VMEM((seq_count, 16, LANES), bf16),
            pltpu.VMEM((blocks * 16, LANES), f32),
            pltpu.VMEM((2 * tall, 2 * tall), bf16),
            pltpu.VMEM((2, 2 * halves, 2 * tall), bf16),
            pltpu.VMEM((filters // 2, tall, 2 * LANES), f32),
            pltpu.VMEM((blocks * 16, LANES), f32),
            pltpu.VMEM((seq_count, 16, LANES), bf16),
            pltpu.VMEM((seq_count, 16, LANES), bf16),
            pltpu.VMEM((8, LANES), f32),
            pltpu.VMEM((ch_count, 8, LANES), f32),
            pltpu.SemaphoreType.DMA((len(operands),)),
            pltpu.SemaphoreType.DMA((5,)),
            pltpu.SemaphoreType.DMA((5,)),
        ],
        compiler_params=pltpu.CompilerParams(
            collective_id=0, has_side_effects=True, vmem_limit_bytes=40 * 1024 * 1024
        ),
        cost_estimate=pl.CostEstimate(
            flops=40 * 2 * 256**3,
            bytes_accessed=4 * local_rows * channels * 2,
            transcendentals=0,
        ),
    )(*operands)


def solution(mesh):
    placed = (P("seq", "ch"), P("seq", "ch"), P("seq", "ch"), P(None, "seq"), P())
    return jax.shard_map(
        local,
        mesh=mesh,
        in_specs=placed,
        out_specs=(P("seq", "ch"), P(None, "seq")),
        check_vma=False,
    )
```

time: 108 us -> 58.3 us (0.54)
  Pallas kernels: 102 us -> 45.3 us
  local copies, waits for them, and re-layouts: 5.27 us -> 11.9 us
    pallas_call x1, Pallas kernels: 102 us -> 45.3 us  [local(): pl.pallas_call(functools.partial(kernel, seq_count, ch_count), out_shape=...]
    unnamed x12 -> x26, local copies, waits for them, and re-layouts: 5.27 us -> 11.9 us
where the time goes in v2:
time: 58.3 us; the launch traced here: 57.8 us
  Pallas kernels  45.3 us (78%)
  local copies, waits for them, and re-layouts  11.9 us (20%)
  between operations  0.66 us (1%)
    pallas_call x1, Pallas kernels, local(): pl.pallas_call(functools.partial(kernel, seq_count, ch_count), out_shape=...  45.3 us
    unnamed x26, local copies, waits for them, and re-layouts  11.9 us

profile of v2, /device:TPU:1, one launch (start us, length us, event | category | flops | bytes accessed | tf_op | source)
XLA Modules:
  0.0 57.8 jit_solution(1403321876529888905)
XLA Ops:
  0.6 0.0 copy-start
  0.6 0.9 %copy-done = bf16[128,512]{1,0:T(8,128)(2,1)S(1)} copy-done((bf16[128,512]{1,0:T(8,128)(2,1)S(1)}, bf16[128,512]{1,0:T(8,128)(2,1)}, u32[]{:S(2)}) %copy-start) | copy-done | bytes 131096
  1.5 0.0 copy-start.1
  1.5 0.9 %copy-done.1 = bf16[128,512]{1,0:T(8,128)(2,1)S(1)} copy-done((bf16[128,512]{1,0:T(8,128)(2,1)S(1)}, bf16[128,512]{1,0:T(8,128)(2,1)}, u32[]{:S(2)}) %copy-start.1) | copy-done | bytes 131096
  2.4 0.0 copy-start.2
  2.4 0.9 %copy-done.2 = bf16[128,512]{1,0:T(8,128)(2,1)S(1)} copy-done((bf16[128,512]{1,0:T(8,128)(2,1)S(1)}, bf16[128,512]{1,0:T(8,128)(2,1)}, u32[]{:S(2)}) %copy-start.2) | copy-done | bytes 131096
  3.3 0.0 copy-start.3
  3.3 0.7 %copy-done.3 = bf16[4,128]{1,0:T(4,128)(2,1)S(1)} copy-done((bf16[4,128]{1,0:T(4,128)(2,1)S(1)}, bf16[4,128]{1,0:T(4,128)(2,1)}, u32[]{:S(2)}) %copy-start.3) | copy-done | bytes 1048
  4.0 0.0 copy-start.4
  4.0 0.7 %copy-done.4 = s32[128]{0:T(128)S(1)} copy-done((s32[128]{0:T(128)S(1)}, s32[128]{0:T(128)}, u32[]{:S(2)}) %copy-start.4) | copy-done | bytes 536
  4.7 0.0 copy-start.5
  4.7 0.9 %copy-done.5 = bf16[2,256,256]{2,1,0:T(8,128)(2,1)S(1)} copy-done((bf16[2,256,256]{2,1,0:T(8,128)(2,1)S(1)}, bf16[2,256,256]{2,1,0:T(8,128)(2,1)}, u32[]{:S(2)}) %copy-start.5) | copy-done | bytes 262168
  5.6 0.0 copy-start.6
  5.6 0.9 %copy-done.6 = bf16[2,256,256]{2,1,0:T(8,128)(2,1)S(1)} copy-done((bf16[2,256,256]{2,1,0:T(8,128)(2,1)S(1)}, bf16[2,256,256]{2,1,0:T(8,128)(2,1)}, u32[]{:S(2)}) %copy-start.6) | copy-done | bytes 262168
  6.6 0.0 copy-start.7
  6.6 0.9 %copy-done.7 = f32[2,256,128]{2,1,0:T(8,128)S(1)} copy-done((f32[2,256,128]{2,1,0:T(8,128)S(1)}, f32[2,256,128]{2,1,0:T(8,128)}, u32[]{:S(2)}) %copy-start.7) | copy-done | bytes 262168
  7.5 0.0 copy-start.8
  7.5 0.9 %copy-done.8 = bf16[2,128,512]{2,1,0:T(8,128)(2,1)S(1)} copy-done((bf16[2,128,512]{2,1,0:T(8,128)(2,1)S(1)}, bf16[2,128,512]{2,1,0:T(8,128)(2,1)}, u32[]{:S(2)}) %copy-start.8) | copy-done | bytes 262168
  8.5 0.9 %copy-done.9 = bf16[512,256]{1,0:T(8,128)(2,1)S(1)} copy-done((bf16[512,256]{1,0:T(8,128)(2,1)S(1)}, bf16[512,256]{1,0:T(8,128)(2,1)}, u32[]{:S(2)}) %copy-start.9) | copy-done | bytes 262168
  9.4 0.9 %copy-done.10 = bf16[128,1024]{1,0:T(8,128)(2,1)S(1)} copy-done((bf16[128,1024]{1,0:T(8,128)(2,1)S(1)}, bf16[128,1024]{1,0:T(8,128)(2,1)}, u32[]{:S(2)}) %copy-start.10) | copy-done | bytes 262168
  10.4 0.9 %copy-done.11 = bf16[1024,128]{1,0:T(8,128)(2,1)S(1)} copy-done((bf16[1024,128]{1,0:T(8,128)(2,1)S(1)}, bf16[1024,128]{1,0:T(8,128)(2,1)}, u32[]{:S(2)}) %copy-start.11) | copy-done | bytes 262168
  11.3 45.3 %shard_map.131 = (bf16[128,512]{1,0:T(8,128)(2,1)S(1)}, f32[4,128]{1,0:T(4,128)S(1)}) custom-call(bf16[128,512]{1,0:T(8,128)(2,1)S(1)} %copy-done, bf16[128,512]{1,0:T(8,128)(2,1)S(1)} %copy-done.1, bf16[128,512]{1,0:T(8,128)(2,1)S(1)} %copy-done.2, bf16[4,128]{1,0:T(4,128)(2,1)S(1)} %copy-done.3, s32[128]{0:T(128)S(1)} %copy-done.4, ...), custom_call_target="tpu_custom_call" | custom-call | flops 1342177280 | bytes 524288 | tf_op jit(solution)/shard_map/pallas_call | solution.py:404
  56.6 0.7 %copy.16 = bf16[128,512]{1,0:T(8,128)(2,1)} copy(bf16[128,512]{1,0:T(8,128)(2,1)S(1)} %get-tuple-element.4) | data formatting | bytes 262144
  57.3 0.6 copy.17
  (3 shorter events, 0.0 us)
Async XLA Ops:
  0.6 0.9 %copy-start = (bf16[128,512]{1,0:T(8,128)(2,1)S(1)}, bf16[128,512]{1,0:T(8,128)(2,1)}, u32[]{:S(2)}) copy-start(bf16[128,512]{1,0:T(8,128)(2,1)} %up_hbm.1) | copy-start | bytes 393220
  1.5 0.9 %copy-start.1 = (bf16[128,512]{1,0:T(8,128)(2,1)S(1)}, bf16[128,512]{1,0:T(8,128)(2,1)}, u32[]{:S(2)}) copy-start(bf16[128,512]{1,0:T(8,128)(2,1)} %gate_hbm.1) | copy-start | bytes 393220
  2.4 0.9 %copy-start.2 = (bf16[128,512]{1,0:T(8,128)(2,1)S(1)}, bf16[128,512]{1,0:T(8,128)(2,1)}, u32[]{:S(2)}) copy-start(bf16[128,512]{1,0:T(8,128)(2,1)} %value_hbm.1) | copy-start | bytes 393220
  3.3 0.7 %copy-start.3 = (bf16[4,128]{1,0:T(4,128)(2,1)S(1)}, bf16[4,128]{1,0:T(4,128)(2,1)}, u32[]{:S(2)}) copy-start(bf16[4,128]{1,0:T(4,128)(2,1)} %taps_hbm.1) | copy-start | bytes 3076
  4.0 0.7 %copy-start.4 = (s32[128]{0:T(128)S(1)}, s32[128]{0:T(128)}, u32[]{:S(2)}) copy-start(s32[128]{0:T(128)} %ids_hbm.1) | copy-start | bytes 1540
  4.7 0.9 %copy-start.5 = (bf16[2,256,256]{2,1,0:T(8,128)(2,1)S(1)}, bf16[2,256,256]{2,1,0:T(8,128)(2,1)}, u32[]{:S(2)}) copy-start(bf16[2,256,256]{2,1,0:T(8,128)(2,1)} %constant.20.clone.outer_hbm) | copy-start | bytes 786436
  5.6 0.9 %copy-start.6 = (bf16[2,256,256]{2,1,0:T(8,128)(2,1)S(1)}, bf16[2,256,256]{2,1,0:T(8,128)(2,1)}, u32[]{:S(2)}) copy-start(bf16[2,256,256]{2,1,0:T(8,128)(2,1)} %constant.19.clone.inner_hbm) | copy-start | bytes 786436
  6.6 0.9 %copy-start.7 = (f32[2,256,128]{2,1,0:T(8,128)S(1)}, f32[2,256,128]{2,1,0:T(8,128)}, u32[]{:S(2)}) copy-start(f32[2,256,128]{2,1,0:T(8,128)} %constant.18.clone.twiddle_hbm) | copy-start | bytes 786436
  7.5 0.9 %copy-start.8 = (bf16[2,128,512]{2,1,0:T(8,128)(2,1)S(1)}, bf16[2,128,512]{2,1,0:T(8,128)(2,1)}, u32[]{:S(2)}) copy-start(bf16[2,128,512]{2,1,0:T(8,128)(2,1)} %constant.17.clone.lags_hbm) | copy-start | bytes 786436
  8.5 0.9 %copy-start.9 = (bf16[512,256]{1,0:T(8,128)(2,1)S(1)}, bf16[512,256]{1,0:T(8,128)(2,1)}, u32[]{:S(2)}) copy-start(bf16[512,256]{1,0:T(8,128)(2,1)} %constant.16.clone.taps_tab_hbm) | copy-start | bytes 786436
  9.4 0.9 %copy-start.10 = (bf16[128,1024]{1,0:T(8,128)(2,1)S(1)}, bf16[128,1024]{1,0:T(8,128)(2,1)}, u32[]{:S(2)}) copy-start(bf16[128,1024]{1,0:T(8,128)(2,1)} %constant.15.clone.back_hbm) | copy-start | bytes 786436
  10.4 0.9 %copy-start.11 = (bf16[1024,128]{1,0:T(8,128)(2,1)S(1)}, bf16[1024,128]{1,0:T(8,128)(2,1)}, u32[]{:S(2)}) copy-start(bf16[1024,128]{1,0:T(8,128)(2,1)} %constant.14.clone.forward_hbm) | copy-start | bytes 786436

commit v3 on v2

--- a/solution.py
+++ b/solution.py
@@ -28,21 +28,21 @@
     angle = 2 * np.pi * np.outer(np.arange(tall), np.arange(halves)) / tall
     cosine, sine = np.cos(angle), -np.sin(angle)
     parts = two_parts(cosine) + two_parts(sine)
-    forward = np.concatenate(parts, 0)
-    back = np.ascontiguousarray(np.concatenate(parts, 0).T)
+    forward = np.concatenate([np.concatenate(parts[0:2], 0), np.concatenate(parts[2:4], 0)], 1)
+    back = np.concatenate([part.T for part in parts], 0)
     natural = np.concatenate([np.arange(0, halves, 2), np.arange(1, halves, 2)])
     both = np.concatenate([cosine, sine], 0)[:, natural]
     taps = np.concatenate(two_parts(both), 1)
-    lags = np.stack(two_parts(np.ascontiguousarray(both.T)))
+    lags = np.concatenate(two_parts(cosine.T[natural]) + two_parts(sine.T[natural]), 0)
     turn = 2 * np.pi * np.outer(np.arange(tall), np.arange(HALF)) / points
     turn = np.tile(turn, (1, 2))
     twiddle = np.stack([np.cos(turn), -np.sin(turn)]).astype(np.float32)
     small = 2 * np.pi * np.outer(np.arange(HALF), np.arange(HALF)) / HALF
     pair = np.eye(2)
     real, imag = np.kron(pair, np.cos(small)), np.kron(pair, -np.sin(small))
-    inner = np.stack(two_parts(np.block([[real, imag], [-imag, real]])))
-    outer = np.stack(two_parts(np.block([[real, -imag], [imag, real]])))
-    return forward, back, taps, lags, twiddle, inner, outer
+    inner = two_parts(np.block([[real, imag], [-imag, real]]))
+    outer = two_parts(np.block([[real, -imag], [imag, real]]))
+    return twiddle, (forward, back, taps, lags) + inner + outer
 
 
 def kernel(
@@ -53,13 +53,8 @@
     value_hbm,
     taps_hbm,
     ids_hbm,
-    forward_hbm,
-    back_hbm,
-    taps_tab_hbm,
-    lags_hbm,
     twiddle_hbm,
-    inner_hbm,
-    outer_hbm,
+    matrix_hbm,
     vg_ref,
     fg_ref,
     up_ref,
@@ -67,13 +62,8 @@
     value_ref,
     taps_ref,
     ids_ref,
-    forward,
-    back,
-    taps_tab,
-    lags_tab,
     twiddle,
-    inner,
-    outer,
+    matrix,
     row_taps,
     packed_taps,
     all_taps,
@@ -110,13 +100,8 @@
         (value_hbm, value_ref),
         (taps_hbm, taps_ref),
         (ids_hbm, ids_ref),
-        (forward_hbm, forward),
-        (back_hbm, back),
-        (taps_tab_hbm, taps_tab),
-        (lags_hbm, lags_tab),
         (twiddle_hbm, twiddle),
-        (inner_hbm, inner),
-        (outer_hbm, outer),
+        (matrix_hbm, matrix),
     )
     loads = [
         pltpu.make_async_copy(src, dst, load_sems.at[i]) for i, (src, dst) in enumerate(pairs)
@@ -221,18 +206,35 @@
     ids = ids_ref[...].reshape(1, halves).astype(f32).astype(bf16)
     split_ids = jnp.dot(ids, split, preferred_element_type=f32).astype(jnp.int32)
     place = jnp.where(slot == split_ids, 1.0, 0.0)
-    sorted_cols = jnp.dot(forward[...], place.astype(bf16), preferred_element_type=f32)
-    sorted_rows = jnp.dot(place.T.astype(bf16), back[...], preferred_element_type=f32)
+    chooser, chooser_rows = place.astype(bf16), place.T.astype(bf16)
+
+    def table(start, rows, first=0, columns=tall):
+        return matrix[start : start + rows, first : first + columns]
+
     for n in range(2):
-        cosine, sine = sorted_cols[n * tall : (n + 1) * tall], sorted_cols[(n + 2) * tall : (n + 3) * tall]
+        cosine = jnp.dot(table(n * tall, tall, 0, halves), chooser, preferred_element_type=f32)
+        sine = jnp.dot(table(n * tall, tall, halves, halves), chooser, preferred_element_type=f32)
         left[0:tall, n * tall : (n + 1) * tall] = jnp.concatenate([cosine, -sine], axis=1).astype(bf16)
         left[tall : 2 * tall, n * tall : (n + 1) * tall] = jnp.concatenate([sine, cosine], axis=1).astype(
             bf16
         )
-        cosine = sorted_rows[:, n * tall : (n + 1) * tall]
-        sine = sorted_rows[:, (n + 2) * tall : (n + 3) * tall]
+        start = 2 * tall + n * halves
+        cosine = jnp.dot(chooser_rows, table(start, halves), preferred_element_type=f32)
+        sine = jnp.dot(chooser_rows, table(start + tall, halves), preferred_element_type=f32)
         left_back[n, 0:halves, :] = jnp.concatenate([cosine, sine], axis=1).astype(bf16)
         left_back[n, halves : 2 * halves, :] = jnp.concatenate([-sine, cosine], axis=1).astype(bf16)
+
+    taps_tab = table(4 * tall, 2 * tall)
+    start = 6 * tall
+    lags_tab = [
+        jnp.concatenate(
+            [table(start + n * halves, halves), table(start + tall + n * halves, halves)], axis=1
+        )
+        for n in range(2)
+    ]
+    inner_rows, outer_rows = 8 * tall, 8 * tall + 4 * LANES
+    inner = [table(inner_rows + n * 2 * LANES, 2 * LANES, 0, 2 * LANES) for n in range(2)]
+    outer = [table(outer_rows + n * 2 * LANES, 2 * LANES, 0, 2 * LANES) for n in range(2)]
 
     low_lane = lax.broadcasted_iota(jnp.int32, (blocks, LANES), 1) < HALF
 
@@ -292,7 +294,7 @@
     taps_in = jnp.concatenate(
         [by_halves(taps_of(f), taps_of(f + 1)) for f in range(0, filters, 2)], axis=1
     ).astype(bf16)
-    taps_first = dot(taps_tab[...], jnp.concatenate([taps_in, taps_in], axis=0))
+    taps_first = dot(taps_tab, jnp.concatenate([taps_in, taps_in], axis=0))
     for q in range(filters // 2):
         lanes = slice(q * LANES, (q + 1) * LANES)
         spectra[q] = spectrum(taps_first[0:tall, lanes], taps_first[tall:, lanes])
@@ -398,7 +400,10 @@
     tall = 2 * halves
     y_count = 1 << ((seq_count.bit_length() - 1) // 2)
     f32, bf16 = jnp.float32, jnp.bfloat16
-    constants = [jnp.asarray(table) for table in tables(halves)]
+    twiddle, pieces = tables(halves)
+    width = max(tall, 2 * LANES)
+    matrix = np.concatenate([np.pad(x, ((0, 0), (0, width - x.shape[1]))) for x in pieces], 0)
+    constants = [jnp.asarray(twiddle), jnp.asarray(matrix)]
     vmem = pl.BlockSpec(memory_space=pltpu.VMEM)
     operands = [upstream_grad, gate_act, value_act, filter_taps, half_ids] + constants
     return pl.pallas_call(
@@ -430,7 +435,7 @@
             pltpu.SemaphoreType.DMA((5,)),
         ],
         compiler_params=pltpu.CompilerParams(
-            collective_id=0, has_side_effects=True, vmem_limit_bytes=40 * 1024 * 1024
+            collective_id=0, has_side_effects=True, vmem_limit_bytes=60 * 1024 * 1024
         ),
         cost_estimate=pl.CostEstimate(
             flops=40 * 2 * 256**3,

time: 58.3 us -> 48.9 us (0.84)
  local copies, waits for them, and re-layouts: 11.9 us -> 2.83 us
    unnamed x26 -> x2, local copies, waits for them, and re-layouts: 11.9 us -> 2.83 us
where the time goes in v3:
time: 48.9 us; the launch traced here: 48.7 us
  Pallas kernels  45.3 us (93%)
  local copies, waits for them, and re-layouts  2.83 us (6%)
  between operations  0.64 us (1%)
    pallas_call x1, Pallas kernels, local(): pl.pallas_call(functools.partial(kernel, seq_count, ch_count), out_shape=...  45.3 us
    unnamed x2, local copies, waits for them, and re-layouts  2.83 us

profile of v3, /device:TPU:1, one launch (start us, length us, event | category | flops | bytes accessed | tf_op | source)
XLA Modules:
  0.0 48.7 jit_solution(14130860025793575427)
XLA Ops:
  0.6 45.3 %shard_map.86 = (bf16[128,512]{1,0:T(8,128)(2,1)}, f32[4,128]{1,0:T(4,128)}) custom-call(bf16[128,512]{1,0:T(8,128)(2,1)} %up_hbm.1, bf16[128,512]{1,0:T(8,128)(2,1)} %gate_hbm.1, bf16[128,512]{1,0:T(8,128)(2,1)} %value_hbm.1, bf16[4,128]{1,0:T(4,128)(2,1)} %taps_hbm.1, s32[128]{0:T(128)} %ids_hbm.1, f32[2,256,128]{2,1,0:T(8,128)} %constant.4.clone.twiddle_hbm, ...), custom_call_target="tpu_custom_call" | custom-call | flops 1342177280 | bytes 524288 | tf_op jit(solution)/shard_map/pallas_call | solution.py:409
  45.9 1.6 %copy.11 = bf16[128,512]{1,0:T(8,128)(2,1)} copy(bf16[128,512]{1,0:T(8,128)(2,1)} %get-tuple-element.4) | data formatting | bytes 262144
  47.5 1.3 %copy.12 = f32[4,128]{1,0:T(4,128)} copy(f32[4,128]{1,0:T(4,128)} %get-tuple-element.5) | data formatting | bytes 4096

commit v4 on v3

--- a/solution.py
+++ b/solution.py
@@ -72,8 +72,8 @@
     wide1,
     left,
     left_back,
-    spectra,
-    wide2,
+    lag_send,
+    lag_recv,
     send2,
     recv2,
     part,
@@ -109,26 +109,23 @@
     for load in loads:
         load.start()
 
-    def partner(d):
-        z = lax.rem(my_z + lax.div(d, y_count), z_count)
-        y = lax.rem(my_y + lax.rem(d, y_count), y_count)
-        return z * y_count + y
+    steps = sorted(
+        ((dz, dy) for dz in range(z_count) for dy in range(y_count) if dz + dy > 0),
+        key=lambda step: -min(step[0], z_count - step[0]) - min(step[1], y_count - step[1]),
+    )
+    partners = [
+        lax.rem(my_z + dz, z_count) * y_count + lax.rem(my_y + dy, y_count) for dz, dy in steps
+    ]
 
     barrier = pltpu.get_barrier_semaphore()
 
-    def greet(d, carry):
-        pl.semaphore_signal(barrier, inc=1, device_id={"seq": partner(d)}, device_id_type=MESH)
-        return carry
-
-    lax.fori_loop(1, seq_count, greet, 0)
-
-    def greet_ch(d, carry):
+    for to in partners:
+        pl.semaphore_signal(barrier, inc=1, device_id={"seq": to}, device_id_type=MESH)
+
+    for d in range(1, ch_count):
         pl.semaphore_signal(
             barrier, inc=1, device_id={"ch": lax.rem(my_ch + d, ch_count)}, device_id_type=MESH
         )
-        return carry
-
-    lax.fori_loop(1, ch_count, greet_ch, 0)
 
     for load in loads[0:4]:
         load.wait()
@@ -160,8 +157,7 @@
 
     lax.fori_loop(1, y_count, send_y, 0)
 
-    def send_first(d, carry):
-        to = partner(d)
+    for to in partners:
         pltpu.make_async_remote_copy(
             src_ref=send1.at[to],
             dst_ref=recv1.at[me],
@@ -170,9 +166,6 @@
             device_id={"seq": to},
             device_id_type=MESH,
         ).start()
-        return carry
-
-    lax.fori_loop(1, seq_count, send_first, 0)
     recv1[me] = send1[me]
 
     def wait_all(ref, sem):
@@ -284,20 +277,6 @@
         re, im = y[:, 0:LANES], y[:, LANES:]
         cosine, sine = twiddle[0], twiddle[1]
         return jnp.concatenate([re * cosine + im * sine, im * cosine - re * sine], axis=0)
-
-    wait_all(all_taps.at[pl.ds(0, z_count - 1)], recv_sems.at[2])
-    taps_wide = all_taps[...].astype(f32)
-
-    def taps_of(f):
-        return taps_wide[:, f * y_count : (f + 1) * y_count, :].reshape(blocks, LANES)
-
-    taps_in = jnp.concatenate(
-        [by_halves(taps_of(f), taps_of(f + 1)) for f in range(0, filters, 2)], axis=1
-    ).astype(bf16)
-    taps_first = dot(taps_tab, jnp.concatenate([taps_in, taps_in], axis=0))
-    for q in range(filters // 2):
-        lanes = slice(q * LANES, (q + 1) * LANES)
-        spectra[q] = spectrum(taps_first[0:tall, lanes], taps_first[tall:, lanes])
 
     wait_all(recv1.at[pl.ds(0, seq_count - 1)], recv_sems.at[1])
     wide1[...] = recv1[...].astype(f32).reshape(blocks * 16, LANES)
@@ -318,29 +297,52 @@
 
     grad_first = first_stage(0)
     value_first = first_stage(8)
-    grad_back, lag_back = [], []
+    grad_spectra, lag_back = [], []
     for q in range(filters // 2):
         lanes = slice(q * LANES, (q + 1) * LANES)
         grad_spec = spectrum(grad_first[0:tall, lanes], grad_first[tall:, lanes])
         value_spec = spectrum(value_first[0:tall, lanes], value_first[tall:, lanes])
-        grad_back.append(unturned(conj_times(spectra[q], grad_spec)))
+        grad_spectra.append(grad_spec)
         lag_back.append(unturned(conj_times(value_spec, grad_spec)))
+    lag_sums = product_left(lags_tab, jnp.concatenate(lag_back, axis=1)) * scale
+
+    for q in range(filters // 2):
+        for n, rows in enumerate(joined(lag_sums[:, q * LANES : (q + 1) * LANES])):
+            lag_send[:, 2 * q + n, :] = rows
+    for to in partners:
+        pltpu.make_async_remote_copy(
+            src_ref=lag_send.at[to],
+            dst_ref=lag_recv.at[me],
+            send_sem=send_sems.at[5],
+            recv_sem=recv_sems.at[5],
+            device_id={"seq": to},
+            device_id_type=MESH,
+        ).start()
+    lag_recv[me] = lag_send[me]
+
+    wait_all(all_taps.at[pl.ds(0, z_count - 1)], recv_sems.at[2])
+    taps_wide = all_taps[...].astype(f32)
+
+    def taps_of(f):
+        return taps_wide[:, f * y_count : (f + 1) * y_count, :].reshape(blocks, LANES)
+
+    taps_in = jnp.concatenate(
+        [by_halves(taps_of(f), taps_of(f + 1)) for f in range(0, filters, 2)], axis=1
+    ).astype(bf16)
+    taps_first = dot(taps_tab, jnp.concatenate([taps_in, taps_in], axis=0))
+    grad_back = []
+    for q in range(filters // 2):
+        lanes = slice(q * LANES, (q + 1) * LANES)
+        taps_spec = spectrum(taps_first[0:tall, lanes], taps_first[tall:, lanes])
+        grad_back.append(unturned(conj_times(taps_spec, grad_spectra[q])))
+
     in_grad = product_left(left_back, jnp.concatenate(grad_back, axis=1)) * scale
-    lag_sums = product_left(lags_tab, jnp.concatenate(lag_back, axis=1)) * scale
-
     for q in range(filters // 2):
         lanes = slice(q * LANES, (q + 1) * LANES)
         for a in range(2):
             for n, rows in enumerate(joined(in_grad[a * halves : (a + 1) * halves, lanes])):
-                wide2[pl.ds(a * filters + 2 * q + n, blocks, stride=16), :] = rows
-        for n, rows in enumerate(joined(lag_sums[:, lanes])):
-            rounded = rows.astype(bf16).astype(f32)
-            wide2[pl.ds(8 + 2 * q + n, blocks, stride=16), :] = rounded
-            wide2[pl.ds(8 + filters + 2 * q + n, blocks, stride=16), :] = rows - rounded
-    send2[...] = wide2[...].reshape(blocks, 16, LANES).astype(bf16)
-
-    def send_back(d, carry):
-        to = partner(d)
+                send2[:, a * filters + 2 * q + n, :] = rows
+    for to in partners:
         pltpu.make_async_remote_copy(
             src_ref=send2.at[to],
             dst_ref=recv2.at[me],
@@ -349,19 +351,11 @@
             device_id={"seq": to},
             device_id_type=MESH,
         ).start()
-        return carry
-
-    lax.fori_loop(1, seq_count, send_back, 0)
     recv2[me] = send2[me]
-    wait_all(recv2.at[pl.ds(0, seq_count - 1)], recv_sems.at[3])
-
-    def add_lags(p, total):
-        return total + recv2[p].astype(f32)
-
-    summed = lax.fori_loop(0, seq_count, add_lags, jnp.zeros((16, LANES), f32))
-    part[...] = summed[8:16]
-
-    def send_ch(d, carry):
+
+    wait_all(lag_recv.at[pl.ds(0, seq_count - 1)], recv_sems.at[5])
+    part[...] = jnp.sum(lag_recv[...], axis=0)
+    for d in range(1, ch_count):
         pltpu.make_async_remote_copy(
             src_ref=part,
             dst_ref=parts.at[my_ch],
@@ -370,22 +364,20 @@
             device_id={"ch": lax.rem(my_ch + d, ch_count)},
             device_id_type=MESH,
         ).start()
-        return carry
-
-    lax.fori_loop(1, ch_count, send_ch, 0)
     parts[my_ch] = part[...]
 
+    wait_all(recv2.at[pl.ds(0, seq_count - 1)], recv_sems.at[3])
     for c in range(vg_ref.shape[1] // LANES):
-        rows = recv2[pl.ds(c * group, group)].astype(f32)[:, 0:8, :].reshape(LANES, LANES)
+        rows = recv2[pl.ds(c * group, group)].reshape(LANES, LANES)
         vg_ref[:, pl.ds(c * LANES, LANES)] = rows.T.astype(bf16)
 
     wait_all(parts.at[pl.ds(0, ch_count - 1)], recv_sems.at[4])
-    both = jnp.sum(parts[...], axis=0)
-    fg_ref[...] = both[0:filters] + both[filters : 2 * filters]
+    fg_ref[...] = jnp.sum(parts[...], axis=0)
 
     wait_all(row_taps.at[pl.ds(0, (y_count - 1) * 8)], send_sems.at[0])
     wait_all(send1.at[pl.ds(0, seq_count - 1)], send_sems.at[1])
     wait_all(all_taps.at[pl.ds(0, z_count - 1)], send_sems.at[2])
+    wait_all(lag_send.at[pl.ds(0, seq_count - 1)], send_sems.at[5])
     wait_all(send2.at[pl.ds(0, seq_count - 1)], send_sems.at[3])
     wait_all(parts.at[pl.ds(0, ch_count - 1)], send_sems.at[4])
 
@@ -409,8 +401,8 @@
     return pl.pallas_call(
         functools.partial(kernel, seq_count, ch_count),
         out_shape=(
-            jax.ShapeDtypeStruct((local_rows, channels), bf16),
-            jax.ShapeDtypeStruct((filters, LANES), f32),
+            pltpu.VMEM((local_rows, channels), bf16),
+            pltpu.VMEM((filters, LANES), f32),
         ),
         in_specs=[pl.BlockSpec(memory_space=pl.ANY)] * len(operands),
         out_specs=(vmem, vmem),
@@ -424,15 +416,15 @@
             pltpu.VMEM((blocks * 16, LANES), f32),
             pltpu.VMEM((2 * tall, 2 * tall), bf16),
             pltpu.VMEM((2, 2 * halves, 2 * tall), bf16),
-            pltpu.VMEM((filters // 2, tall, 2 * LANES), f32),
-            pltpu.VMEM((blocks * 16, LANES), f32),
-            pltpu.VMEM((seq_count, 16, LANES), bf16),
-            pltpu.VMEM((seq_count, 16, LANES), bf16),
-            pltpu.VMEM((8, LANES), f32),
-            pltpu.VMEM((ch_count, 8, LANES), f32),
+            pltpu.VMEM((seq_count, filters, LANES), f32),
+            pltpu.VMEM((seq_count, filters, LANES), f32),
+            pltpu.VMEM((seq_count, 8, LANES), f32),
+            pltpu.VMEM((seq_count, 8, LANES), f32),
+            pltpu.VMEM((filters, LANES), f32),
+            pltpu.VMEM((ch_count, filters, LANES), f32),
             pltpu.SemaphoreType.DMA((len(operands),)),
-            pltpu.SemaphoreType.DMA((5,)),
-            pltpu.SemaphoreType.DMA((5,)),
+            pltpu.SemaphoreType.DMA((6,)),
+            pltpu.SemaphoreType.DMA((6,)),
         ],
         compiler_params=pltpu.CompilerParams(
             collective_id=0, has_side_effects=True, vmem_limit_bytes=60 * 1024 * 1024

time: 48.9 us -> 43.2 us (0.88)
  Pallas kernels: 45.3 us -> 41.2 us
  local copies, waits for them, and re-layouts: 2.83 us -> 1.24 us
    pallas_call x1, Pallas kernels: 45.3 us -> 41.2 us  [local(): pl.pallas_call(functools.partial(kernel, seq_count, ch_count), out_shape=...]
    unnamed x2, local copies, waits for them, and re-layouts: 2.83 us -> 1.24 us
where the time goes in v4:
time: 43.2 us; the launch traced here: 43.1 us
  Pallas kernels  41.2 us (95%)
  local copies, waits for them, and re-layouts  1.24 us (3%)
  between operations  0.64 us (1%)
    pallas_call x1, Pallas kernels, local(): pl.pallas_call(functools.partial(kernel, seq_count, ch_count), out_shape=...  41.2 us
    unnamed x2, local copies, waits for them, and re-layouts  1.24 us

profile of v4, /device:TPU:1, one launch (start us, length us, event | category | flops | bytes accessed | tf_op | source)
XLA Modules:
  0.0 43.1 jit_solution(2150499887007612461)
XLA Ops:
  0.6 41.2 %shard_map.86 = (bf16[128,512]{1,0:T(8,128)(2,1)S(1)}, f32[4,128]{1,0:T(4,128)S(1)}) custom-call(bf16[128,512]{1,0:T(8,128)(2,1)} %up_hbm.1, bf16[128,512]{1,0:T(8,128)(2,1)} %gate_hbm.1, bf16[128,512]{1,0:T(8,128)(2,1)} %value_hbm.1, bf16[4,128]{1,0:T(4,128)(2,1)} %taps_hbm.1, s32[128]{0:T(128)} %ids_hbm.1, f32[2,256,128]{2,1,0:T(8,128)} %constant.4.clone.twiddle_hbm, ...), custom_call_target="tpu_custom_call" | custom-call | flops 1342177280 | bytes 524288 | tf_op jit(solution)/shard_map/pallas_call | solution.py:401
  41.8 0.7 %copy.11 = bf16[128,512]{1,0:T(8,128)(2,1)} copy(bf16[128,512]{1,0:T(8,128)(2,1)S(1)} %get-tuple-element.2) | data formatting | bytes 262144
  42.5 0.6 %copy.12 = f32[4,128]{1,0:T(4,128)} copy(f32[4,128]{1,0:T(4,128)S(1)} %get-tuple-element.3) | data formatting | bytes 4096

commit v5 on v4

--- a/solution.py
+++ b/solution.py
@@ -25,16 +25,17 @@
 def tables(halves):
     tall = 2 * halves
     points = tall * HALF
-    angle = 2 * np.pi * np.outer(np.arange(tall), np.arange(halves)) / tall
+    angle = 2 * np.pi * np.outer(np.arange(halves), np.arange(halves)) / tall
     cosine, sine = np.cos(angle), -np.sin(angle)
-    parts = two_parts(cosine) + two_parts(sine)
-    forward = np.concatenate([np.concatenate(parts[0:2], 0), np.concatenate(parts[2:4], 0)], 1)
-    back = np.concatenate([part.T for part in parts], 0)
+    sine[0] = np.cos(np.pi * np.arange(halves))
+    both = np.concatenate([cosine, sine], 0)
     natural = np.concatenate([np.arange(0, halves, 2), np.arange(1, halves, 2)])
-    both = np.concatenate([cosine, sine], 0)[:, natural]
-    taps = np.concatenate(two_parts(both), 1)
-    lags = np.concatenate(two_parts(cosine.T[natural]) + two_parts(sine.T[natural]), 0)
-    turn = 2 * np.pi * np.outer(np.arange(tall), np.arange(HALF)) / points
+    forward = np.concatenate(two_parts(both), 1)
+    back = np.concatenate(two_parts(both.T), 0)
+    taps = np.concatenate(two_parts(both[:, natural]), 1)
+    lags = np.concatenate(two_parts(both.T[natural]), 0)
+    order = np.concatenate([np.arange(halves + 1), np.arange(tall - 1, halves, -1)])
+    turn = 2 * np.pi * np.outer(order, np.arange(HALF)) / points
     turn = np.tile(turn, (1, 2))
     twiddle = np.stack([np.cos(turn), -np.sin(turn)]).astype(np.float32)
     small = 2 * np.pi * np.outer(np.arange(HALF), np.arange(HALF)) / HALF
@@ -205,31 +206,21 @@
         return matrix[start : start + rows, first : first + columns]
 
     for n in range(2):
-        cosine = jnp.dot(table(n * tall, tall, 0, halves), chooser, preferred_element_type=f32)
-        sine = jnp.dot(table(n * tall, tall, halves, halves), chooser, preferred_element_type=f32)
-        left[0:tall, n * tall : (n + 1) * tall] = jnp.concatenate([cosine, -sine], axis=1).astype(bf16)
-        left[tall : 2 * tall, n * tall : (n + 1) * tall] = jnp.concatenate([sine, cosine], axis=1).astype(
-            bf16
-        )
-        start = 2 * tall + n * halves
-        cosine = jnp.dot(chooser_rows, table(start, halves), preferred_element_type=f32)
-        sine = jnp.dot(chooser_rows, table(start + tall, halves), preferred_element_type=f32)
-        left_back[n, 0:halves, :] = jnp.concatenate([cosine, sine], axis=1).astype(bf16)
-        left_back[n, halves : 2 * halves, :] = jnp.concatenate([-sine, cosine], axis=1).astype(bf16)
-
-    taps_tab = table(4 * tall, 2 * tall)
-    start = 6 * tall
-    lags_tab = [
-        jnp.concatenate(
-            [table(start + n * halves, halves), table(start + tall + n * halves, halves)], axis=1
-        )
-        for n in range(2)
-    ]
-    inner_rows, outer_rows = 8 * tall, 8 * tall + 4 * LANES
+        left[:, n * halves : (n + 1) * halves] = jnp.dot(
+            table(0, tall, n * halves, halves), chooser, preferred_element_type=f32
+        ).astype(bf16)
+        left_back[n] = jnp.dot(
+            chooser_rows, table(tall + n * halves, halves), preferred_element_type=f32
+        ).astype(bf16)
+
+    taps_tab = table(2 * tall, tall)
+    lags_tab = [table(3 * tall + n * halves, halves) for n in range(2)]
+    inner_rows, outer_rows = 4 * tall, 4 * tall + 4 * LANES
     inner = [table(inner_rows + n * 2 * LANES, 2 * LANES, 0, 2 * LANES) for n in range(2)]
     outer = [table(outer_rows + n * 2 * LANES, 2 * LANES, 0, 2 * LANES) for n in range(2)]
 
     low_lane = lax.broadcasted_iota(jnp.int32, (blocks, LANES), 1) < HALF
+    top_row = lax.broadcasted_iota(jnp.int32, (halves, LANES), 0) == 0
 
     def by_halves(rows0, rows1):
         return jnp.concatenate(
@@ -276,34 +267,55 @@
         y = product_right(x, outer)
         re, im = y[:, 0:LANES], y[:, LANES:]
         cosine, sine = twiddle[0], twiddle[1]
-        return jnp.concatenate([re * cosine + im * sine, im * cosine - re * sine], axis=0)
+        re, im = re * cosine + im * sine, im * cosine - re * sine
+        re, re_pair, im, im_pair = re[0:halves], re[halves:], im[0:halves], im[halves:]
+        real = [jnp.where(top_row, re, re + re_pair), jnp.where(top_row, re_pair, im - im_pair)]
+        imag = [jnp.where(top_row, im, im + im_pair), jnp.where(top_row, im_pair, re_pair - re)]
+        return jnp.concatenate(real, axis=0), jnp.concatenate(imag, axis=0)
+
+    def unfolded(of_real, of_imag=None):
+        cos_re, sin_re = of_real[0:halves], of_real[halves:]
+        sin_low = jnp.where(top_row, 0.0, sin_re)
+        if of_imag is None:
+            re = [cos_re, jnp.where(top_row, sin_re, cos_re)]
+            im = [sin_low, -sin_low]
+        else:
+            cos_im, sin_im = of_imag[0:halves], of_imag[halves:]
+            re = [
+                cos_re - jnp.where(top_row, 0.0, sin_im),
+                jnp.where(top_row, sin_re, cos_re + sin_im),
+            ]
+            im = [cos_im + sin_low, jnp.where(top_row, sin_im, cos_im - sin_re)]
+        return jnp.concatenate(re, axis=0), jnp.concatenate(im, axis=0)
 
     wait_all(recv1.at[pl.ds(0, seq_count - 1)], recv_sems.at[1])
     wide1[...] = recv1[...].astype(f32).reshape(blocks * 16, LANES)
 
     def first_stage(base):
-        columns = []
-        for f in range(0, filters, 2):
-            rows = [
+        data = jnp.concatenate(
+            [
                 by_halves(
                     wide1[pl.ds(base + a * filters + f, blocks, stride=16), :],
                     wide1[pl.ds(base + a * filters + f + 1, blocks, stride=16), :],
                 )
                 for a in range(2)
-            ]
-            columns.append(jnp.concatenate(rows, axis=0))
-        data = jnp.concatenate(columns, axis=1).astype(bf16)
+                for f in range(0, filters, 2)
+            ],
+            axis=1,
+        ).astype(bf16)
         return dot(left[...], jnp.concatenate([data, data], axis=0))
 
     grad_first = first_stage(0)
     value_first = first_stage(8)
+    pairs_of_filters = filters // 2
     grad_spectra, lag_back = [], []
-    for q in range(filters // 2):
-        lanes = slice(q * LANES, (q + 1) * LANES)
-        grad_spec = spectrum(grad_first[0:tall, lanes], grad_first[tall:, lanes])
-        value_spec = spectrum(value_first[0:tall, lanes], value_first[tall:, lanes])
+    for q in range(pairs_of_filters):
+        real = slice(q * LANES, (q + 1) * LANES)
+        imag = slice((pairs_of_filters + q) * LANES, (pairs_of_filters + q + 1) * LANES)
+        grad_spec = spectrum(*unfolded(grad_first[:, real], grad_first[:, imag]))
+        value_spec = spectrum(*unfolded(value_first[:, real], value_first[:, imag]))
         grad_spectra.append(grad_spec)
-        lag_back.append(unturned(conj_times(value_spec, grad_spec)))
+        lag_back.append(unturned(conj_times(value_spec, grad_spec))[0])
     lag_sums = product_left(lags_tab, jnp.concatenate(lag_back, axis=1)) * scale
 
     for q in range(filters // 2):
@@ -333,14 +345,15 @@
     grad_back = []
     for q in range(filters // 2):
         lanes = slice(q * LANES, (q + 1) * LANES)
-        taps_spec = spectrum(taps_first[0:tall, lanes], taps_first[tall:, lanes])
+        taps_spec = spectrum(*unfolded(taps_first[:, lanes]))
         grad_back.append(unturned(conj_times(taps_spec, grad_spectra[q])))
 
-    in_grad = product_left(left_back, jnp.concatenate(grad_back, axis=1)) * scale
-    for q in range(filters // 2):
-        lanes = slice(q * LANES, (q + 1) * LANES)
-        for a in range(2):
-            for n, rows in enumerate(joined(in_grad[a * halves : (a + 1) * halves, lanes])):
+    folded = [grad_back[q][a] for a in range(2) for q in range(pairs_of_filters)]
+    in_grad = product_left(left_back, jnp.concatenate(folded, axis=1)) * scale
+    for a in range(2):
+        for q in range(pairs_of_filters):
+            start = (a * pairs_of_filters + q) * LANES
+            for n, rows in enumerate(joined(in_grad[:, start : start + LANES])):
                 send2[:, a * filters + 2 * q + n, :] = rows
     for to in partners:
         pltpu.make_async_remote_copy(
@@ -380,6 +393,11 @@
     wait_all(lag_send.at[pl.ds(0, seq_count - 1)], send_sems.at[5])
     wait_all(send2.at[pl.ds(0, seq_count - 1)], send_sems.at[3])
     wait_all(parts.at[pl.ds(0, ch_count - 1)], send_sems.at[4])
+
+
+def write_out(vg_ref, fg_ref, vg_out, fg_out):
+    vg_out[...] = vg_ref[...]
+    fg_out[...] = fg_ref[...]
 
 
 def local(upstream_grad, gate_act, value_act, filter_taps, half_ids):
@@ -398,7 +416,7 @@
     constants = [jnp.asarray(twiddle), jnp.asarray(matrix)]
     vmem = pl.BlockSpec(memory_space=pltpu.VMEM)
     operands = [upstream_grad, gate_act, value_act, filter_taps, half_ids] + constants
-    return pl.pallas_call(
+    results = pl.pallas_call(
         functools.partial(kernel, seq_count, ch_count),
         out_shape=(
             pltpu.VMEM((local_rows, channels), bf16),
@@ -414,8 +432,8 @@
             pltpu.VMEM((seq_count, 16, LANES), bf16),
             pltpu.VMEM((seq_count, 16, LANES), bf16),
             pltpu.VMEM((blocks * 16, LANES), f32),
-            pltpu.VMEM((2 * tall, 2 * tall), bf16),
-            pltpu.VMEM((2, 2 * halves, 2 * tall), bf16),
+            pltpu.VMEM((tall, tall), bf16),
+            pltpu.VMEM((2, halves, tall), bf16),
             pltpu.VMEM((seq_count, filters, LANES), f32),
             pltpu.VMEM((seq_count, filters, LANES), f32),
             pltpu.VMEM((seq_count, 8, LANES), f32),
@@ -435,6 +453,16 @@
             transcendentals=0,
         ),
     )(*operands)
+    return pl.pallas_call(
+        write_out,
+        out_shape=(
+            jax.ShapeDtypeStruct((local_rows, channels), bf16),
+            jax.ShapeDtypeStruct((filters, LANES), f32),
+        ),
+        in_specs=[vmem, vmem],
+        out_specs=(vmem, vmem),
+        compiler_params=pltpu.CompilerParams(vmem_limit_bytes=1024 * 1024),
+    )(*results)
 
 
 def solution(mesh):

time: 43.2 us -> 42.5 us (0.984)
  local copies, waits for them, and re-layouts: 1.24 us -> 0 us
  Pallas kernels: 41.2 us -> 41.7 us
    unnamed x2 -> x0, local copies, waits for them, and re-layouts: 1.24 us -> none
    pallas_call x0 -> x1, Pallas kernels: none -> 0.67 us  [local(): pl.pallas_call(write_out, out_shape=(jax.ShapeDtypeStruct((local_rows, ch...]
where the time goes in v5:
time: 42.5 us; the launch traced here: 42.3 us
  Pallas kernels  41.7 us (98%)
  between operations  0.64 us (2%)
    pallas_call x1, Pallas kernels, local(): pl.pallas_call(functools.partial(kernel, seq_count, ch_count), out_shape=...  41 us

profile of v5, /device:TPU:1, one launch (start us, length us, event | category | flops | bytes accessed | tf_op | source)
XLA Modules:
  0.0 42.3 jit_solution(984802772606440865)
XLA Ops:
  0.6 41.0 %shard_map.86 = (bf16[128,512]{1,0:T(8,128)(2,1)S(1)}, f32[4,128]{1,0:T(4,128)S(1)}) custom-call(bf16[128,512]{1,0:T(8,128)(2,1)} %up_hbm.1, bf16[128,512]{1,0:T(8,128)(2,1)} %gate_hbm.1, bf16[128,512]{1,0:T(8,128)(2,1)} %value_hbm.1, bf16[4,128]{1,0:T(4,128)(2,1)} %taps_hbm.1, s32[128]{0:T(128)} %ids_hbm.1, f32[2,256,128]{2,1,0:T(8,128)} %constant.4.clone.twiddle_hbm, ...), custom_call_target="tpu_custom_call" | custom-call | flops 1342177280 | bytes 524288 | tf_op jit(solution)/shard_map/pallas_call | solution.py:419
  41.7 0.7 %shard_map.87 = (bf16[128,512]{1,0:T(8,128)(2,1)}, f32[4,128]{1,0:T(4,128)}) custom-call(bf16[128,512]{1,0:T(8,128)(2,1)S(1)} %get-tuple-element.4.vg_ref, f32[4,128]{1,0:T(4,128)S(1)} %get-tuple-element.5.fg_ref), custom_call_target="tpu_custom_call" | custom-call | tf_op jit(solution)/shard_map/pallas_call | solution.py:456

commit v6 on v5

--- a/solution.py
+++ b/solution.py
@@ -355,7 +355,7 @@
             start = (a * pairs_of_filters + q) * LANES
             for n, rows in enumerate(joined(in_grad[:, start : start + LANES])):
                 send2[:, a * filters + 2 * q + n, :] = rows
-    for to in partners:
+    for to in partners[::-1]:
         pltpu.make_async_remote_copy(
             src_ref=send2.at[to],
             dst_ref=recv2.at[me],

time: 42.5 us -> 42.3 us (level)
  no operation moved by 1% of the time
where the time goes in v6:
time: 42.3 us; the launch traced here: 42.2 us
  Pallas kernels  41.5 us (98%)
  between operations  0.64 us (2%)
    pallas_call x1, Pallas kernels, local(): pl.pallas_call(functools.partial(kernel, seq_count, ch_count), out_shape=...  40.9 us

profile of v6, /device:TPU:1, one launch (start us, length us, event | category | flops | bytes accessed | tf_op | source)
XLA Modules:
  0.0 42.2 jit_solution(1170481197066836678)
XLA Ops:
  0.6 40.9 %shard_map.86 = (bf16[128,512]{1,0:T(8,128)(2,1)S(1)}, f32[4,128]{1,0:T(4,128)S(1)}) custom-call(bf16[128,512]{1,0:T(8,128)(2,1)} %up_hbm.1, bf16[128,512]{1,0:T(8,128)(2,1)} %gate_hbm.1, bf16[128,512]{1,0:T(8,128)(2,1)} %value_hbm.1, bf16[4,128]{1,0:T(4,128)(2,1)} %taps_hbm.1, s32[128]{0:T(128)} %ids_hbm.1, f32[2,256,128]{2,1,0:T(8,128)} %constant.4.clone.twiddle_hbm, ...), custom_call_target="tpu_custom_call" | custom-call | flops 1342177280 | bytes 524288 | tf_op jit(solution)/shard_map/pallas_call | solution.py:419
  41.5 0.7 %shard_map.87 = (bf16[128,512]{1,0:T(8,128)(2,1)}, f32[4,128]{1,0:T(4,128)}) custom-call(bf16[128,512]{1,0:T(8,128)(2,1)S(1)} %get-tuple-element.4.vg_ref, f32[4,128]{1,0:T(4,128)S(1)} %get-tuple-element.5.fg_ref), custom_call_target="tpu_custom_call" | custom-call | tf_op jit(solution)/shard_map/pallas_call | solution.py:456

commit v7 on v5

--- a/solution.py
+++ b/solution.py
@@ -367,7 +367,8 @@
     recv2[me] = send2[me]
 
     wait_all(lag_recv.at[pl.ds(0, seq_count - 1)], recv_sems.at[5])
-    part[...] = jnp.sum(lag_recv[...], axis=0)
+    sums = jnp.sum(lag_recv[...].reshape(seq_count // 2, 2 * filters, LANES), axis=0)
+    part[...] = sums[0:filters] + sums[filters:]
     for d in range(1, ch_count):
         pltpu.make_async_remote_copy(
             src_ref=part,

time: 42.5 us -> 42.4 us (level)
  no operation moved by 1% of the time
where the time goes in v7:
time: 42.4 us; the launch traced here: 42.3 us
  Pallas kernels  41.7 us (98%)
  between operations  0.64 us (2%)
    pallas_call x1, Pallas kernels, local(): pl.pallas_call(functools.partial(kernel, seq_count, ch_count), out_shape=...  41 us

profile of v7, /device:TPU:1, one launch (start us, length us, event | category | flops | bytes accessed | tf_op | source)
XLA Modules:
  0.0 42.3 jit_solution(2178539856482905669)
XLA Ops:
  0.6 41.0 %shard_map.86 = (bf16[128,512]{1,0:T(8,128)(2,1)S(1)}, f32[4,128]{1,0:T(4,128)S(1)}) custom-call(bf16[128,512]{1,0:T(8,128)(2,1)} %up_hbm.1, bf16[128,512]{1,0:T(8,128)(2,1)} %gate_hbm.1, bf16[128,512]{1,0:T(8,128)(2,1)} %value_hbm.1, bf16[4,128]{1,0:T(4,128)(2,1)} %taps_hbm.1, s32[128]{0:T(128)} %ids_hbm.1, f32[2,256,128]{2,1,0:T(8,128)} %constant.4.clone.twiddle_hbm, ...), custom_call_target="tpu_custom_call" | custom-call | flops 1342177280 | bytes 524288 | tf_op jit(solution)/shard_map/pallas_call | solution.py:420
  41.6 0.7 %shard_map.87 = (bf16[128,512]{1,0:T(8,128)(2,1)}, f32[4,128]{1,0:T(4,128)}) custom-call(bf16[128,512]{1,0:T(8,128)(2,1)S(1)} %get-tuple-element.4.vg_ref, f32[4,128]{1,0:T(4,128)S(1)} %get-tuple-element.5.fg_ref), custom_call_target="tpu_custom_call" | custom-call | tf_op jit(solution)/shard_map/pallas_call | solution.py:457
